TPU v7x, 512 devices: a whole 4x4x16 slice. The times are simulated.
512 devices in a mesh: pool: 16 (over x, y), dcp: 32 (over z, core).
Axes of the slice: x: 4, y: 4, z: 16, core: 2. Of those that a mesh axis runs over, the one named last changes fastest.
Arguments:
- q_latent: bfloat16 [16, 4, 64, 512], P('pool'), may hold values from -70 to 70
- q_rope: bfloat16 [16, 4, 4096], P('pool'), may hold values from -6 to 6
- pool_latent: bfloat16 [24576, 64, 512], P(('pool', 'dcp')), may hold values from -6 to 6
- pool_rope: bfloat16 [24576, 4096], P(('pool', 'dcp')), may hold values from -6 to 6
- page_table: int32 [16, 1536], replicated, may hold values from -1 to 24575, as said below
- lengths: int32 [16], replicated, may hold values from 1 to 98304, as said below
- slot_request: int32 [16], replicated, may hold values from 0 to 15, each once
Outputs:
- context: bfloat16 [16, 4, 64, 512], P('pool', None, 'dcp')
- log_total: float32 [16, 4, 64], P('pool', None, 'dcp')
Inputs may be any that keep to these rules, and one draw needn't show every extreme that they name: `page_table`: entry k of row r is -1 exactly when k * 64 >= lengths[r], else a row of pool_latent; no row is named twice. Row index // 48 is the device that holds it (pool index times the size of dcp plus dcp index). Each device holds at most 3 pages of one request, and exactly 3 pages of the longest request. `lengths`: one request has 98304 tokens.
All inputs are finite; a program needn't handle non-finite values.
Results may differ from a plain program's by a relative error of at most 0.003.
Values may be sent and summed in bfloat16 or wider, within the bound.
A program may use at most 64 MiB of HBM per device.

v0:
```python
import jax
import jax.numpy as jnp
from jax import lax
from jax.sharding import PartitionSpec as P

QK_NOPE = 128


NEGATIVE = -1e30


def lookup(values_table, wanted_index):
    positions = jnp.arange(values_table.shape[0], dtype=jnp.int32)
    return jnp.sum(jnp.where(positions == wanted_index, values_table, 0))


def per_device(q_latent, q_rope, pool_latent, pool_rope, page_table, lengths, slot_request):
    pool_width = lax.axis_size("pool")
    context_width = lax.axis_size("dcp")
    pool_index = lax.axis_index("pool")
    member = lax.axis_index("dcp")
    device = pool_index * context_width + member
    slot_count, page_size, latent_width = pool_latent.shape
    rope_width = pool_rope.shape[1] // page_size
    capacity = slot_count // pool_width
    per_member = page_size // context_width
    longest = page_table.shape[1]
    request_count = page_table.shape[0]
    chooser = slot_request[:, None] == jnp.arange(request_count, dtype=jnp.int32)[None, :]
    served = jnp.sum(jnp.where(chooser[:, :, None], page_table[None, :, :], 0), axis=1)
    holder = jnp.floor_divide(served, slot_count)
    held_here = (served >= 0) & (holder == device)
    ranked = jnp.cumsum(held_here.astype(jnp.int32), axis=1) - 1
    wanted = held_here[:, None, :] & (
        ranked[:, None, :] == jnp.arange(capacity, dtype=jnp.int32)[None, :, None]
    )
    local_slot = jnp.sum(jnp.where(wanted, (served % slot_count)[:, None, :], 0), axis=2)
    page_index = jnp.arange(longest, dtype=jnp.int32)
    present = jnp.any(wanted, axis=2)
    page_number = jnp.where(
        present, jnp.sum(jnp.where(wanted, page_index[None, None, :], 0), axis=2), -1
    )
    picked = local_slot.reshape(-1)
    latent_out = pool_latent[picked].reshape(
        pool_width, capacity, per_member, context_width, latent_width
    )
    latent_out = latent_out.transpose(0, 1, 3, 2, 4).reshape(
        pool_width, capacity, context_width, per_member * latent_width
    )
    rope_out = pool_rope[picked].reshape(
        pool_width, capacity, per_member, context_width, rope_width
    )
    rope_out = rope_out.transpose(0, 1, 3, 2, 4).reshape(
        pool_width, capacity, context_width, per_member * rope_width
    )
    pages_out = jnp.broadcast_to(page_number[:, :, None], (pool_width, capacity, context_width))
    latent_in, rope_in, pages_in = (
        lax.all_to_all(
            lax.all_to_all(latent_out, "pool", split_axis=0, concat_axis=0, tiled=True),
            "dcp",
            split_axis=2,
            concat_axis=2,
            tiled=True,
        ),
        lax.all_to_all(
            lax.all_to_all(rope_out, "pool", split_axis=0, concat_axis=0, tiled=True),
            "dcp",
            split_axis=2,
            concat_axis=2,
            tiled=True,
        ),
        lax.all_to_all(
            lax.all_to_all(pages_out, "pool", split_axis=0, concat_axis=0, tiled=True),
            "dcp",
            split_axis=2,
            concat_axis=2,
            tiled=True,
        ),
    )
    request = lookup(slot_request, pool_index)
    length = lookup(lengths, request)
    offsets = jnp.arange(per_member, dtype=jnp.int32) * context_width + member
    position = pages_in[..., None] * page_size + offsets
    usable = ((pages_in[..., None] >= 0) & (position < length)).reshape(-1)
    cached = latent_in.reshape(-1, latent_width)
    key_rope = rope_in.reshape(-1, rope_width)
    query_count = q_latent.shape[1]
    head_count = q_latent.shape[2]
    queries = q_latent.reshape(query_count * head_count, latent_width)
    query_rope = q_rope.reshape(query_count * head_count, rope_width)
    factor = (QK_NOPE + rope_width) ** (-0.5)
    contract = (((1,), (1,)), ((), ()))
    scores = lax.dot_general(queries, cached, contract, preferred_element_type=jnp.float32)
    scores = (
        scores + lax.dot_general(query_rope, key_rope, contract, preferred_element_type=jnp.float32)
    ) * factor
    scores = jnp.where(usable[None, :], scores, NEGATIVE)
    part_top = jnp.max(scores, axis=1)
    weights = jnp.where(usable[None, :], jnp.exp(scores - part_top[:, None]), 0.0).astype(
        jnp.bfloat16
    )
    part_total = jnp.sum(weights.astype(jnp.float32), axis=1)
    part_blend = jnp.dot(weights, cached, preferred_element_type=jnp.float32)
    head_share = head_count // context_width
    start = member * head_share
    top_score = lax.pmax(part_top, "dcp")
    rescale = jnp.exp(part_top - top_score)
    blended = part_blend * rescale[:, None]
    totals = part_total * rescale
    blended, totals = lax.psum((blended, totals), "dcp")
    blended = lax.dynamic_slice_in_dim(
        blended.reshape(query_count, head_count, latent_width), start, head_share, 1
    )
    totals = lax.dynamic_slice_in_dim(totals.reshape(query_count, head_count), start, head_share, 1)
    top_share = lax.dynamic_slice_in_dim(
        top_score.reshape(query_count, head_count), start, head_share, 1
    )
    context = (blended / totals[..., None]).astype(jnp.bfloat16)[None]
    log_total = (top_share + jnp.log(totals))[None]
    return (context, log_total)


def solution(mesh):
    in_specs = (
        P("pool", None, None, None),
        P("pool", None, None),
        P(("pool", "dcp"), None, None),
        P(("pool", "dcp"), None),
        P(),
        P(),
        P(),
    )
    out_specs = (P("pool", None, "dcp", None), P("pool", None, "dcp"))
    return jax.shard_map(
        per_device, mesh=mesh, in_specs=in_specs, out_specs=out_specs, check_vma=False
    )
```

profile of v0, /device:TPU:1, one launch (start us, length us, event | category | flops | bytes accessed | tf_op | source)
XLA Modules:
  0.0 616.2 jit_solution(5630003563927620100)
XLA Ops:
  8.1 1.4 select_reduce_fusion
  10.8 1.6 fusion.10
  12.5 1.4 and.58
  13.9 1.4 ge.23
  15.3 1.5 div.23
  16.8 1.6 fusion.7
  18.4 9.4 %reduce-window.6 = s32[16,12,128]{2,1,0:T(8,128)} reduce-window(s32[16,12,128]{2,1,0:T(8,128)} %fusion.7, s32[]{:T(128)} %constant.16.clone.1), window={size=1x1x128 pad=0_0x0_0x127_0}, to_apply=%region_1.2 | reduce-window | flops 3121152 | bytes 196612 | tf_op jit(solution)/shard_map/reduce-window
  27.8 1.3 slice_reduce_fusion
  29.3 1.0 add_add_fusion
  30.4 0.9 fusion.4
  31.3 1.2 select_reduce_fusion.2
  33.2 7.6 %all-to-all-start = ((s32[16,3,32]{2,1,0:T(4,128)}), s32[16,3,32]{2,1,0:T(4,128)}, u32[]{:S(2)}, u32[]{:S(2)}) async-start(s32[16,3,32]{2,1,0:T(4,128)} %broadcast_in_dim.106), calls=%async_computation | async-start | bytes 65536 | tf_op jit(solution)/shard_map/all_to_all | solution.py:73
  41.1 6.3 %all-to-all-done = s32[16,3,32]{2,1,0:T(4,128)} async-done(((s32[16,3,32]{2,1,0:T(4,128)}), s32[16,3,32]{2,1,0:T(4,128)}, u32[]{:S(2)}, u32[]{:S(2)}) %all-to-all-start) | async-done | bytes 6176 | tf_op jit(solution)/shard_map/all_to_all | solution.py:73
  47.4 1.5 copy.53
  48.9 17.4 %all-to-all-start.1 = ((s32[16,3,32]{0,1,2:T(4,128)}), s32[16,3,32]{0,1,2:T(4,128)}, u32[]{:S(2)}, u32[]{:S(2)}) async-start(s32[16,3,32]{0,1,2:T(4,128)} %copy.53), calls=%async_computation.1 | async-start | bytes 131072 | tf_op jit(solution)/shard_map/all_to_all | solution.py:72
  66.3 1.5 gather_fusion.1
  67.8 2.6 reshape.197
  70.5 2.8 copy.71
  73.3 2.7 reshape.198
  76.0 3.4 all-to-all-done.1
  79.4 3.6 all-to-all-start.4
  83.0 2.5 gather_fusion
  85.5 6.9 %copy.70 = bf16[16,3,2,32,512]{4,2,3,1,0:T(2,128)(2,1)} copy(bf16[16,3,2,32,512]{4,3,2,1,0:T(8,128)(2,1)} %bitcast.30) | data formatting | bytes 6291456 | tf_op jit(solution)/shard_map/reshape | solution.py:44
  92.3 6.1 reshape.194
  98.4 6.6 %all-to-all-start.2 = ((bf16[16,3,32,1024]{3,2,1,0:T(8,128)(2,1)}), bf16[16,3,32,1024]{3,2,1,0:T(8,128)(2,1)}, u32[]{:S(2)}, u32[]{:S(2)}) async-start(bf16[16,3,32,1024]{3,2,1,0:T(8,128)(2,1)} %reshape.194), calls=%async_computation.2 | async-start | bytes 6291456 | tf_op jit(solution)/shard_map/all_to_all | solution.py:59
  105.1 0.9 copy.63
  106.0 35.8 %all-to-all-done.2 = bf16[16,3,32,1024]{3,2,1,0:T(8,128)(2,1)} async-done(((bf16[16,3,32,1024]{3,2,1,0:T(8,128)(2,1)}), bf16[16,3,32,1024]{3,2,1,0:T(8,128)(2,1)}, u32[]{:S(2)}, u32[]{:S(2)}) %all-to-all-start.2) | async-done | bytes 3145760 | tf_op jit(solution)/shard_map/all_to_all | solution.py:59
  141.8 15.2 %all-to-all-start.5 = ((bf16[16,3,32,128]{3,0,1,2:T(8,128)(2,1)}), bf16[16,3,32,128]{3,0,1,2:T(8,128)(2,1)S(1)}, u32[]{:S(2)}, u32[]{:S(2)}) async-start(bf16[16,3,32,128]{3,0,1,2:T(8,128)(2,1)} %copy.63), calls=%async_computation.5 | async-start | bytes 786432 | tf_op jit(solution)/shard_map/all_to_all | solution.py:65
  157.0 5.3 copy.60
  162.3 22.7 %all-to-all-done.5 = bf16[16,3,32,128]{3,0,1,2:T(8,128)(2,1)S(1)} async-done(((bf16[16,3,32,128]{3,0,1,2:T(8,128)(2,1)}), bf16[16,3,32,128]{3,0,1,2:T(8,128)(2,1)S(1)}, u32[]{:S(2)}, u32[]{:S(2)}) %all-to-all-start.5) | async-done | bytes 393248 | tf_op jit(solution)/shard_map/all_to_all | solution.py:65
  184.9 4.9 all-to-all-start.3
  189.9 1.5 reshape.200
  192.0 1.3 fusion.14
  193.3 1.5 copy.54
  196.3 1.9 fusion.2
  198.2 1.4 and.63
  200.5 2.2 reshape.199
  202.8 128.6 %all-to-all-done.3 = bf16[16,3,32,1024]{3,0,1,2:T(8,128)(2,1)} async-done(((bf16[16,3,32,1024]{3,0,1,2:T(8,128)(2,1)}), bf16[16,3,32,1024]{3,0,1,2:T(8,128)(2,1)}, u32[]{:S(2)}, u32[]{:S(2)}) %all-to-all-start.3) | async-done | bytes 3145760 | tf_op jit(solution)/shard_map/all_to_all | solution.py:58
  331.3 5.3 copy.61
  336.7 5.7 reshape.195
  342.4 3.0 fusion.19
  345.4 2.8 fusion.18
  348.2 50.4 %pmax.7 = f32[256]{0:T(256)S(1)} all-reduce(f32[256]{0:T(256)S(1)} %get-tuple-element.13), channel_id=1, replica_groups=mesh['pool'=16,'dcp'=32] {'dcp'}, use_global_device_ids=true, to_apply=%region_9.10 | all-reduce | flops 256 | bytes 2048 | tf_op jit(solution)/shard_map/pmax | solution.py:106
  398.6 3.1 convert_reduce_fusion
  401.8 4.6 convolution_multiply_fusion
  406.6 45.8 %psum.15 = f32[4,64]{1,0:T(4,128)S(1)} all-reduce(f32[4,64]{1,0:T(4,128)S(1)} %reshape.202), channel_id=1, replica_groups=mesh['pool'=16,'dcp'=32] {'dcp'}, use_global_device_ids=true, to_apply=%region_12.13 | all-reduce | flops 256 | bytes 2048 | tf_op jit(solution)/shard_map/psum | solution.py:110
  453.1 154.7 %all-reduce.2.cloned.1.call-done = f32[4,64,512]{2,1,0:T(8,128)} async-done(((f32[4,64,512]{2,1,0:T(8,128)}), f32[4,64,512]{2,1,0:T(8,128)}) %all-reduce.2.cloned.1.call-update) | async-done | bytes 524304 | tf_op jit(solution)/shard_map/psum | solution.py:110
  607.8 1.5 fusion.12
  (44 shorter events, 7.4 us)
Async XLA Ops:
  7.2 75.8 %copy-start = (bf16[48,64,512]{2,1,0:T(8,128)(2,1)S(1)}, bf16[48,64,512]{2,1,0:T(8,128)(2,1)}, u32[]{:S(2)}) copy-start(bf16[48,64,512]{2,1,0:T(8,128)(2,1)} %param.9) | copy-start | bytes 9437188
  7.2 59.1 %copy-start.1 = (bf16[48,4096]{1,0:T(8,128)(2,1)S(1)}, bf16[48,4096]{1,0:T(8,128)(2,1)}, u32[]{:S(2)}) copy-start(bf16[48,4096]{1,0:T(8,128)(2,1)} %param.10) | copy-start | bytes 1179652
  9.5 0.6 copy-start.4
  33.2 14.2 %all-to-all-start = ((s32[16,3,32]{2,1,0:T(4,128)}), s32[16,3,32]{2,1,0:T(4,128)}, u32[]{:S(2)}, u32[]{:S(2)}) async-start(s32[16,3,32]{2,1,0:T(4,128)} %broadcast_in_dim.106), calls=%async_computation | async-start | bytes 65536 | tf_op jit(solution)/shard_map/all_to_all | solution.py:73
  48.9 30.5 %all-to-all-start.1 = ((s32[16,3,32]{0,1,2:T(4,128)}), s32[16,3,32]{0,1,2:T(4,128)}, u32[]{:S(2)}, u32[]{:S(2)}) async-start(s32[16,3,32]{0,1,2:T(4,128)} %copy.53), calls=%async_computation.1 | async-start | bytes 131072 | tf_op jit(solution)/shard_map/all_to_all | solution.py:72
  79.4 19.0 %all-to-all-start.4 = ((bf16[16,3,32,128]{3,2,1,0:T(8,128)(2,1)}), bf16[16,3,32,128]{3,2,1,0:T(8,128)(2,1)S(1)}, u32[]{:S(2)}, u32[]{:S(2)}) async-start(bf16[16,3,32,128]{3,2,1,0:T(8,128)(2,1)} %reshape.198), calls=%async_computation.4 | async-start | bytes 786432 | tf_op jit(solution)/shard_map/all_to_all | solution.py:66
  98.4 43.4 %all-to-all-start.2 = ((bf16[16,3,32,1024]{3,2,1,0:T(8,128)(2,1)}), bf16[16,3,32,1024]{3,2,1,0:T(8,128)(2,1)}, u32[]{:S(2)}, u32[]{:S(2)}) async-start(bf16[16,3,32,1024]{3,2,1,0:T(8,128)(2,1)} %reshape.194), calls=%async_computation.2 | async-start | bytes 6291456 | tf_op jit(solution)/shard_map/all_to_all | solution.py:59
  141.8 43.2 %all-to-all-start.5 = ((bf16[16,3,32,128]{3,0,1,2:T(8,128)(2,1)}), bf16[16,3,32,128]{3,0,1,2:T(8,128)(2,1)S(1)}, u32[]{:S(2)}, u32[]{:S(2)}) async-start(bf16[16,3,32,128]{3,0,1,2:T(8,128)(2,1)} %copy.63), calls=%async_computation.5 | async-start | bytes 786432 | tf_op jit(solution)/shard_map/all_to_all | solution.py:65
  162.3 29.1 %copy-start.7 = (s32[16]{0:T(128)S(1)}, s32[16]{0:T(128)}, u32[]{:S(2)}) copy-start(s32[16]{0:T(128)} %param.13) | copy-start | bytes 196
  162.3 29.8 %copy-start.8 = (s32[16]{0:T(128)S(1)}, s32[16]{0:T(128)}, u32[]{:S(2)}) copy-start(s32[16]{0:T(128)} %param.12) | copy-start | bytes 196
  184.9 146.4 %all-to-all-start.3 = ((bf16[16,3,32,1024]{3,0,1,2:T(8,128)(2,1)}), bf16[16,3,32,1024]{3,0,1,2:T(8,128)(2,1)}, u32[]{:S(2)}, u32[]{:S(2)}) async-start(bf16[16,3,32,1024]{3,0,1,2:T(8,128)(2,1)} %copy.60), calls=%async_computation.3 | async-start | bytes 6291456 | tf_op jit(solution)/shard_map/all_to_all | solution.py:58
  189.9 418.0 %all-reduce.2.cloned.1.call-start = ((), (), s32[]{:S(2)}) async-start(), calls=%async_computation.6 | async-start | bytes 1048576 | tf_op jit(solution)/shard_map/psum | solution.py:110
  336.6 5.7 copy-start.6
  342.4 3.0 copy-start.3
  342.4 3.0 copy-start.5
  398.6 3.1 copy-start.2
Sparse Core Ops, SparseCore 0:
  406.6 201.2 all-reduce.1
where the time goes:
time: 619 us; the launch traced here: 616 us
  waiting for transfers between devices  352 us (57%)
  blocking collectives  96.2 us (16%)
  local copies, waits for them, and re-layouts  59.6 us (10%)
  starting transfers between devices  55.3 us (9%)
  other arithmetic  28.9 us (5%)
  between operations  14.2 us (2%)
  matrix products  10.4 us (2%)
    psum x1, waiting for transfers between devices, per_device(): blended, totals = lax.psum((blended, totals), 'dcp')  155 us
    all_to_all x1, waiting for transfers between devices, per_device(): lax.all_to_all(lax.all_to_all(latent_out, 'pool', split_axis=0, concat_ax...  129 us
    pmax x1, blocking collectives, per_device(): top_score = lax.pmax(part_top, 'dcp')  50.4 us
    psum x1, blocking collectives, per_device(): blended, totals = lax.psum((blended, totals), 'dcp')  45.8 us
    all_to_all x1, waiting for transfers between devices, per_device(): lax.all_to_all(latent_out, 'pool', split_axis=0, concat_axis=0, tiled=True)  35.8 us
    all_to_all x1, waiting for transfers between devices, per_device(): lax.all_to_all(lax.all_to_all(rope_out, 'pool', split_axis=0, concat_axis...  22.7 us
    all_to_all x1, starting transfers between devices, per_device(): lax.all_to_all(lax.all_to_all(pages_out, 'pool', split_axis=0, concat_axi...  17.4 us
    all_to_all x1, starting transfers between devices, per_device(): lax.all_to_all(lax.all_to_all(rope_out, 'pool', split_axis=0, concat_axis...  15.2 us
  transfers between devices with their start and end apart: 7, of which 6 were waited for; matrix products, arithmetic and copies ran while one was open for 7% of the time, Pallas kernels for 0%

commit v1 on v0

v1 whole, which is shorter than its diff:
```python
import functools

import jax
import jax.numpy as jnp
from jax import lax
from jax.experimental import pallas as pl
from jax.experimental.pallas import tpu as pltpu
from jax.sharding import PartitionSpec as P

MESH = pl.DeviceIdType.MESH
QK_NOPE = 128
NEG = -1e30
EMPTY = -1e29

SIDE = 4
RING = 16
PAGES = 48
CAP = 3
TOK = 64
LAT = 512
ROPE = 64
ROWS = 256
HALF = 128
SPAN = 768
MAXP = 1536

SENDS = (
    (1, 2, 1), (1, 1, 2), (1, 3, 2), (0, 2, 2), (0, 1, 1), (0, 3, 1),
    (1, 2, 0), (1, 1, 3), (1, 3, 3), (0, 2, 3), (0, 1, 0), (0, 3, 0),
)
ORDER = (1, 2, 3, 0)


def dot(a, b):
    return jnp.dot(a, b, preferred_element_type=jnp.float32)


def dot_t(a, b):
    return lax.dot_general(a, b, (((1,), (1,)), ((), ())), preferred_element_type=jnp.float32)


def iota(shape, dim):
    return lax.broadcasted_iota(jnp.int32, shape, dim)


def kernel(
    slot_s, len_s, table, ql, qr, lat_hbm, rope_hbm,
    ctx_out, log_out,
    lat_v, rope_v, rope_f, tab_p, tab_r, idx_v, idx_s,
    stage_l, stage_r, kv, kr, krx, qs, qcat, s_ref, p_ref,
    acc, st, r0_acc, r0_st, h_acc, h_st, r1_acc, r1_st, fin, zbuf,
    load_sem, idx_sem, kv_send, kv_recv, kr_send, kr_recv,
    q_send, q_recv, f_send, f_recv, r0_send, r0_recv, r1_send, r1_recv, z_send, z_recv,
):
    pool = lax.axis_index("pool")
    member = lax.axis_index("dcp")
    px, py = pool // SIDE, pool % SIDE
    z, core = member // 2, member % 2

    def wrap(v):
        return lax.rem(v + 2 * SIDE, SIDE)

    def axes(x, y):
        odd = lax.rem(x + y, 2)
        return ((odd, 1 - odd), (1 - odd, odd))

    def shift(x, y, unit, steps):
        return wrap(x + steps * unit[0]), wrap(y + steps * unit[1])

    def group_at(x, y, place):
        other, key = axes(x, y)
        if place == 0:
            gx, gy = x, y
        elif place == 1:
            gx, gy = shift(x, y, other, 2)
        elif place == 2:
            gx, gy = shift(x, y, key, 1)
        else:
            gx, gy = shift(x, y, key, 3)
        return gx * SIDE + gy

    mine = axes(px, py)

    def peer(axis, steps):
        x, y = shift(px, py, mine[axis], steps)
        return (x * SIDE + y, member)

    sibling = (pool, z * 2 + 1 - core)

    def around(steps):
        return (pool, lax.rem(z + steps, RING) * 2 + core)

    load_l = pltpu.make_async_copy(lat_hbm, lat_v, load_sem.at[0])
    load_r = pltpu.make_async_copy(rope_hbm, rope_v, load_sem.at[1])
    load_r.start()
    load_l.start()

    barrier = pltpu.get_barrier_semaphore()
    greet = [peer(axis, steps) for axis in (0, 1) for steps in (1, 2, 3)]
    greet += [sibling] + [around(steps) for steps in range(1, RING)]
    for device in greet:
        pl.semaphore_signal(barrier, inc=1, device_id=device, device_id_type=MESH)

    device = pool * 32 + member
    for g in range(16):
        tab_p[pl.ds(g, 1), :] = table[pl.ds(slot_s[g], 1), :] - device * PAGES
    groups = [group_at(px, py, a) for a in range(4)]
    for a in range(4):
        row = table[pl.ds(slot_s[groups[a]], 1), :]
        for b in range(4):
            x, y = shift(px, py, mine[1] if a < 2 else mine[0], b)
            tab_r[pl.ds(4 * a + b, 1), :] = row - ((x * SIDE + y) * 32 + member) * PAGES

    def picks(tab):
        local = jnp.where((tab >= 0) & (tab < PAGES), tab, 64)
        found = []
        for _ in range(CAP):
            first = jnp.min(local, axis=1, keepdims=True)
            found.append(first)
            local = jnp.where(local > first, local, 64)
        return found

    def lanes(values):
        lane = iota((16, 128), 1)
        out = jnp.zeros((16, 128), jnp.int32)
        for j in range(CAP):
            out = jnp.where(lane == j, values[j], out)
        return out

    idx_v[0:16, :] = lanes([jnp.minimum(v, PAGES - 1) for v in picks(tab_p[...])])
    tab = tab_r[...]
    page = iota((16, MAXP), 1)
    quarter = iota((16, 1), 0) // 4
    length = jnp.zeros((16, 1), jnp.int32)
    for a in range(4):
        length = jnp.where(quarter == a, len_s[slot_s[groups[a]]], length)
    counts = []
    for first in picks(tab):
        number = jnp.sum(jnp.where(tab == first, page, 0), axis=1, keepdims=True)
        count = jnp.clip(length - number * TOK, 0, TOK)
        counts.append(jnp.where(first < 64, count, 0))
    idx_v[16:32, :] = lanes(counts)
    to_smem = pltpu.make_async_copy(idx_v, idx_s, idx_sem)
    to_smem.start()

    def parts(shape):
        r = iota(shape, 0)
        return r // HALF, (r // 8) % RING, (r // 2) % 4, r % 2

    c_, z_, q_, h_ = parts((ROWS, ROWS))
    perm = (iota((ROWS, ROWS), 1) == q_ * 64 + 4 * z_ + 2 * c_ + h_).astype(jnp.bfloat16)
    qcat[0, :, 0:LAT] = dot(perm, ql[...]).astype(jnp.bfloat16)
    rope_rows = qr[...].astype(jnp.float32)
    for i in range(32):
        qs[4 * i : 4 * i + 4, :] = rope_rows[:, 128 * i : 128 * i + 128]
    c_, z_, q_, h_ = parts((ROWS, 128))
    pick = (iota((ROWS, 128), 1) == (2 * z_ + c_) * 4 + q_).astype(jnp.bfloat16)
    pair = dot(pick, qs[...].astype(jnp.bfloat16))
    swapped = jnp.concatenate([pair[:, 64:128], pair[:, 0:64]], axis=1)
    qcat[0, :, LAT : LAT + 128] = jnp.where(
        iota((ROWS, 128), 1) // 64 == h_, pair, swapped
    ).astype(jnp.bfloat16)

    load_r.wait()
    for i in range(32):
        rope_f[PAGES * i : PAGES * i + PAGES, :] = rope_v[:, 128 * i : 128 * i + 128].astype(
            jnp.float32
        )
    to_smem.wait()
    load_l.wait()

    def take(group, j):
        slot = idx_s[group, j]
        return lat_v[slot], rope_f[pl.ds(slot, 32, stride=PAGES), :].astype(jnp.bfloat16)

    pl.semaphore_wait(barrier, len(greet))

    half = pl.ds(pl.multiple_of(core * HALF, HALF), HALF)
    rest = pl.ds(pl.multiple_of((1 - core) * HALF, HALF), HALF)
    query = {}
    for steps, place in ((1, 3), (3, 2), (2, 1)):
        query[place] = pltpu.make_async_remote_copy(
            src_ref=qcat.at[0, half],
            dst_ref=qcat.at[place, half],
            send_sem=q_send.at[place],
            recv_sem=q_recv.at[place],
            device_id=peer(0, steps),
            device_id_type=MESH,
        )
        query[place].start()

    sent = {}
    for i, (axis, steps, place) in enumerate(SENDS):
        tx, ty = shift(px, py, mine[axis], steps)
        group = group_at(tx, ty, place)
        for j in range(CAP):
            latent, rope = take(group, j)
            stage_l[i, j] = latent
            stage_r[i, j] = rope
        source = 4 - steps
        pair_of = (
            pltpu.make_async_remote_copy(
                src_ref=stage_l.at[i],
                dst_ref=kv.at[place, :, source],
                send_sem=kv_send.at[i],
                recv_sem=kv_recv.at[place, source],
                device_id=(tx * SIDE + ty, member),
                device_id_type=MESH,
            ),
            pltpu.make_async_remote_copy(
                src_ref=stage_r.at[i],
                dst_ref=kr.at[place, :, source],
                send_sem=kr_send.at[i],
                recv_sem=kr_recv.at[place, source],
                device_id=(tx * SIDE + ty, member),
                device_id_type=MESH,
            ),
        )
        for copy in pair_of:
            copy.start()
        sent[place, source] = pair_of

    for a in range(4):
        for j in range(CAP):
            latent, rope = take(groups[a], j)
            kv[a, j, 0] = latent
            kr[a, j, 0] = rope

    passed = {}
    for place in (2, 3, 1):
        query[place].wait_recv()
        passed[place] = pltpu.make_async_remote_copy(
            src_ref=qcat.at[place, half],
            dst_ref=qcat.at[place, half],
            send_sem=f_send.at[place],
            recv_sem=f_recv.at[place],
            device_id=sibling,
            device_id_type=MESH,
        )
        passed[place].start()

    factor = (QK_NOPE + ROPE) ** (-0.5)
    expand = (iota((256, 128), 0) // 2 == iota((256, 128), 1)).astype(jnp.bfloat16)
    parity = iota((256, 128), 1) // 64 == iota((256, 128), 0) % 2
    within = iota((1, 256), 1) % TOK
    source_of = iota((1, 256), 1) // TOK
    lane = iota((HALF, 128), 1)

    def attend(a):
        for j in range(CAP):
            pairs = kr[a, j].reshape(128, 128)
            krx[...] = jnp.where(parity, dot(expand, pairs), 0.0).astype(jnp.bfloat16)
            keys = kv[a, j].reshape(256, LAT)
            scores = dot_t(qcat[a, :, 0:LAT], keys) + dot_t(qcat[a, :, LAT:], krx[...])
            limit = jnp.zeros((1, 256), jnp.int32)
            for b in range(4):
                limit = jnp.where(source_of == b, idx_s[16 + 4 * a + b, j], limit)
            s_ref[:, 256 * j : 256 * j + 256] = jnp.where(within < limit, scores * factor, NEG)
        for block in range(4):
            rows = slice(64 * block, 64 * block + 64)
            s = s_ref[rows, :]
            top = jnp.maximum(jnp.max(s, axis=1, keepdims=True), EMPTY)
            p = jnp.exp(s - top).astype(jnp.bfloat16)
            p_ref[rows, :] = p
            total = jnp.sum(p.astype(jnp.float32), axis=1, keepdims=True)
            l64 = iota((64, 128), 1)
            st[a, rows, :] = jnp.where(l64 == 0, top, jnp.where(l64 == 1, total, 0.0))
        acc[a] = dot(p_ref[...], kv[a].reshape(SPAN, LAT))

    def merge(parts_):
        top = functools.reduce(jnp.maximum, [t for _, t, _ in parts_])
        scales = [jnp.exp(t - top) for _, t, _ in parts_]
        total = sum(w * l for w, (_, _, l) in zip(scales, parts_))
        sums = sum(w * v for w, (v, _, _) in zip(scales, parts_))
        return sums, top, total

    exchange, returned = {}, {}

    def swap(a):
        exchange[a] = (
            pltpu.make_async_remote_copy(
                src_ref=acc.at[a, rest],
                dst_ref=r0_acc.at[a],
                send_sem=r0_send.at[a, 0],
                recv_sem=r0_recv.at[a, 0],
                device_id=sibling,
                device_id_type=MESH,
            ),
            pltpu.make_async_remote_copy(
                src_ref=st.at[a, rest],
                dst_ref=r0_st.at[a],
                send_sem=r0_send.at[a, 1],
                recv_sem=r0_recv.at[a, 1],
                device_id=sibling,
                device_id_type=MESH,
            ),
        )
        for copy in exchange[a]:
            copy.start()

    def halves(a):
        for copy in exchange[a]:
            copy.wait_recv()
        own = st[a, half, :]
        other = r0_st[a]
        return [
            (acc[a, half, :], own[:, 0:1], own[:, 1:2]),
            (r0_acc[a], other[:, 0:1], other[:, 1:2]),
        ]

    def give_back(a):
        sums, top, total = merge(halves(a))
        h_acc[a - 1] = sums
        stats = jnp.where(lane == 0, top, jnp.where(lane == 1, total, 0.0))
        h_st[a - 1] = stats.T[0:8, :]
        axis, steps = {1: (0, 2), 2: (1, 1), 3: (1, 3)}[a]
        slot = {1: 1, 2: 2, 3: 0}[a]
        returned[a] = (
            pltpu.make_async_remote_copy(
                src_ref=h_acc.at[a - 1],
                dst_ref=r1_acc.at[slot],
                send_sem=r1_send.at[slot, 0],
                recv_sem=r1_recv.at[slot, 0],
                device_id=peer(axis, steps),
                device_id_type=MESH,
            ),
            pltpu.make_async_remote_copy(
                src_ref=h_st.at[a - 1],
                dst_ref=r1_st.at[slot],
                send_sem=r1_send.at[slot, 1],
                recv_sem=r1_recv.at[slot, 1],
                device_id=peer(axis, steps),
                device_id_type=MESH,
            ),
        )
        for copy in returned[a]:
            copy.start()

    pending = None
    for a in ORDER:
        if a:
            passed[a].wait_recv()
        for source in (1, 2, 3):
            for copy in sent[a, source]:
                copy.wait_recv()
        attend(a)
        swap(a)
        if pending is not None:
            give_back(pending)
        pending = a

    pieces = halves(0)
    for a in (1, 2, 3):
        for copy in returned[a]:
            copy.wait_recv()
    for slot in range(3):
        back = jnp.concatenate([r1_st[slot], jnp.zeros((120, 128), jnp.float32)], axis=0).T
        pieces.append((r1_acc[slot], back[:, 0:1], back[:, 1:2]))
    sums, top, total = merge(pieces)
    fin[:, 0:LAT] = sums
    fin[:, LAT:] = jnp.where(lane == 0, top, jnp.where(lane == 1, total, 0.0))

    spread = []
    for steps in range(1, RING):
        rows = pl.ds(pl.multiple_of(lax.rem(z + steps, RING) * 8, 8), 8)
        copy = pltpu.make_async_remote_copy(
            src_ref=fin.at[rows],
            dst_ref=zbuf.at[steps],
            send_sem=z_send.at[steps],
            recv_sem=z_recv.at[steps],
            device_id=around(steps),
            device_id_type=MESH,
        )
        copy.start()
        spread.append(copy)
    zbuf[0] = fin[pl.ds(pl.multiple_of(z * 8, 8), 8), :]
    for copy in spread:
        copy.wait_recv()
    pieces = [
        (zbuf[i, :, 0:LAT], zbuf[i, :, LAT : LAT + 1], zbuf[i, :, LAT + 1 : LAT + 2])
        for i in range(RING)
    ]
    sums, top, total = merge(pieces)
    ctx_out[...] = sums / total
    log_out[...] = jnp.broadcast_to(top + jnp.log(total), (8, 128))

    for copy in spread:
        copy.wait_send()
    for place in (1, 2, 3):
        query[place].wait_send()
        passed[place].wait_send()
        for copy in returned[place]:
            copy.wait_send()
    for a in range(4):
        for copy in exchange[a]:
            copy.wait_send()
    for pair_of in sent.values():
        for copy in pair_of:
            copy.wait_send()


def per_device(q_latent, q_rope, pool_latent, pool_rope, page_table, lengths, slot_request):
    vmem = pl.BlockSpec(memory_space=pltpu.VMEM)
    smem = pl.BlockSpec(memory_space=pltpu.SMEM)
    anywhere = pl.BlockSpec(memory_space=pl.ANY)
    f32, bf16, i32 = jnp.float32, jnp.bfloat16, jnp.int32
    dma = pltpu.SemaphoreType.DMA
    ctx, log = pl.pallas_call(
        kernel,
        out_shape=(jax.ShapeDtypeStruct((8, LAT), f32), jax.ShapeDtypeStruct((8, 128), f32)),
        in_specs=[smem, smem, vmem, vmem, vmem, anywhere, anywhere],
        out_specs=(vmem, vmem),
        scratch_shapes=[
            pltpu.VMEM((PAGES, TOK, LAT), bf16),
            pltpu.VMEM((PAGES, TOK * ROPE), bf16),
            pltpu.VMEM((32 * PAGES, 128), f32),
            pltpu.VMEM((16, MAXP), i32),
            pltpu.VMEM((16, MAXP), i32),
            pltpu.VMEM((32, 128), i32),
            pltpu.SMEM((32, 128), i32),
            pltpu.VMEM((12, CAP, TOK, LAT), bf16),
            pltpu.VMEM((12, CAP, 32, 128), bf16),
            pltpu.VMEM((4, CAP, 4, TOK, LAT), bf16),
            pltpu.VMEM((4, CAP, 4, 32, 128), bf16),
            pltpu.VMEM((256, 128), bf16),
            pltpu.VMEM((128, 128), f32),
            pltpu.VMEM((4, ROWS, LAT + 128), bf16),
            pltpu.VMEM((ROWS, SPAN), f32),
            pltpu.VMEM((ROWS, SPAN), bf16),
            pltpu.VMEM((4, ROWS, LAT), f32),
            pltpu.VMEM((4, ROWS, 128), f32),
            pltpu.VMEM((4, HALF, LAT), f32),
            pltpu.VMEM((4, HALF, 128), f32),
            pltpu.VMEM((3, HALF, LAT), f32),
            pltpu.VMEM((3, 8, 128), f32),
            pltpu.VMEM((3, HALF, LAT), f32),
            pltpu.VMEM((3, 8, 128), f32),
            pltpu.VMEM((HALF, LAT + 128), f32),
            pltpu.VMEM((RING, 8, LAT + 128), f32),
            dma((2,)),
            dma,
            dma((12,)),
            dma((4, 4)),
            dma((12,)),
            dma((4, 4)),
            dma((4,)),
            dma((4,)),
            dma((4,)),
            dma((4,)),
            dma((4, 2)),
            dma((4, 2)),
            dma((3, 2)),
            dma((3, 2)),
            dma((RING,)),
            dma((RING,)),
        ],
        compiler_params=pltpu.CompilerParams(
            collective_id=0, has_side_effects=True, vmem_limit_bytes=48 * 2**20
        ),
        cost_estimate=pl.CostEstimate(flops=2 * 10**9, bytes_accessed=4 * 10**6, transcendentals=10**6),
    )(
        slot_request,
        lengths,
        page_table,
        q_latent.reshape(ROWS, LAT),
        q_rope.reshape(4, 64 * ROPE),
        pool_latent,
        pool_rope,
    )
    context = ctx.astype(bf16).reshape(1, 4, 2, LAT)
    return context, log[:, 0].reshape(1, 4, 2)


def solution(mesh):
    in_specs = (
        P("pool", None, None, None),
        P("pool", None, None),
        P(("pool", "dcp"), None, None),
        P(("pool", "dcp"), None),
        P(),
        P(),
        P(),
    )
    out_specs = (P("pool", None, "dcp", None), P("pool", None, "dcp"))
    return jax.shard_map(
        per_device, mesh=mesh, in_specs=in_specs, out_specs=out_specs, check_vma=False
    )
```

time: 619 us -> 83.1 us (0.13)
  the two profiles are of different devices: /device:TPU:1 before, /device:TPU:10 now
where the time goes in v1:
time: 83.1 us; the launch traced here: 82.8 us
  Pallas kernels  73.9 us (89%)
  local copies, waits for them, and re-layouts  8.25 us (10%)
    pallas_call x1, Pallas kernels, per_device(): pl.pallas_call(kernel, out_shape=(jax.ShapeDtypeStruct((8, LAT), f32), ja...  73.9 us
    unnamed x15, local copies, waits for them, and re-layouts  7.44 us

profile of v1, /device:TPU:10, one launch (start us, length us, event | category | flops | bytes accessed | tf_op | source)
XLA Modules:
  0.0 82.8 jit_solution(6964653423090360927)
XLA Ops:
  0.6 0.0 copy-start
  0.6 1.9 %copy-done = bf16[48,64,512]{2,1,0:T(8,128)(2,1)S(1)} copy-done((bf16[48,64,512]{2,1,0:T(8,128)(2,1)S(1)}, bf16[48,64,512]{2,1,0:T(8,128)(2,1)}, u32[]{:S(2)}) %copy-start) | copy-done | bytes 3145752
  2.5 0.0 copy-start.1
  2.5 1.0 %copy-done.1 = bf16[48,4096]{1,0:T(8,128)(2,1)S(1)} copy-done((bf16[48,4096]{1,0:T(8,128)(2,1)S(1)}, bf16[48,4096]{1,0:T(8,128)(2,1)}, u32[]{:S(2)}) %copy-start.1) | copy-done | bytes 393240
  3.5 0.0 copy-start.2
  3.5 0.9 %copy-done.2 = bf16[1,4,64,512]{3,2,1,0:T(8,128)(2,1)S(1)} copy-done((bf16[1,4,64,512]{3,2,1,0:T(8,128)(2,1)S(1)}, bf16[1,4,64,512]{3,2,1,0:T(8,128)(2,1)}, u32[]{:S(2)}) %copy-start.2) | copy-done | bytes 262168
  4.5 0.0 copy-start.3
  4.5 0.9 %copy-done.3 = s32[16,1536]{1,0:T(8,128)S(1)} copy-done((s32[16,1536]{1,0:T(8,128)S(1)}, s32[16,1536]{1,0:T(8,128)}, u32[]{:S(2)}) %copy-start.3) | copy-done | bytes 98328
  5.4 0.0 copy-start.4
  5.4 0.8 copy-done.4
  6.1 0.0 copy-start.5
  6.1 0.7 copy-done.5
  6.8 0.0 copy-start.6
  6.8 0.7 copy-done.6
  7.4 73.9 %shard_map.86 = (f32[8,512]{1,0:T(8,128)S(1)}, f32[8,128]{1,0:T(8,128)S(1)}) custom-call(s32[16]{0:T(128)S(1)} %copy-done.5, s32[16]{0:T(128)S(1)} %copy-done.6, s32[16,1536]{1,0:T(8,128)S(1)} %copy-done.3, bf16[256,512]{1,0:T(8,128)(2,1)S(1)} %bitcast.2, bf16[4,4096]{1,0:T(4,128)(2,1)S(1)} %bitcast.3, bf16[48,64,512]{2,1,0:T(8,128)(2,1)S(1)} %copy-done, ...), custom_call_target="tpu_custom_call" | custom-call | flops 2000000000 | bytes 4000000 | tf_op jit(solution)/shard_map/pallas_call | solution.py:408
  81.3 0.6 reshape.15
  81.9 0.1 slice_reduce_fusion
  82.0 0.1 reshape_squeeze.3
  82.1 0.7 copy.10
  (1 shorter events, 0.0 us)
Async XLA Ops:
  0.6 1.9 %copy-start = (bf16[48,64,512]{2,1,0:T(8,128)(2,1)S(1)}, bf16[48,64,512]{2,1,0:T(8,128)(2,1)}, u32[]{:S(2)}) copy-start(bf16[48,64,512]{2,1,0:T(8,128)(2,1)} %lat_hbm.1) | copy-start | bytes 9437188
  2.5 1.0 %copy-start.1 = (bf16[48,4096]{1,0:T(8,128)(2,1)S(1)}, bf16[48,4096]{1,0:T(8,128)(2,1)}, u32[]{:S(2)}) copy-start(bf16[48,4096]{1,0:T(8,128)(2,1)} %rope_hbm.1) | copy-start | bytes 1179652
  3.5 0.9 %copy-start.2 = (bf16[1,4,64,512]{3,2,1,0:T(8,128)(2,1)S(1)}, bf16[1,4,64,512]{3,2,1,0:T(8,128)(2,1)}, u32[]{:S(2)}) copy-start(bf16[1,4,64,512]{3,2,1,0:T(8,128)(2,1)} %param.7) | copy-start | bytes 786436
  4.5 0.9 %copy-start.3 = (s32[16,1536]{1,0:T(8,128)S(1)}, s32[16,1536]{1,0:T(8,128)}, u32[]{:S(2)}) copy-start(s32[16,1536]{1,0:T(8,128)} %table.1) | copy-start | bytes 294916
  5.4 0.8 copy-start.4
  6.1 0.7 copy-start.5
  6.8 0.7 copy-start.6

commit v2 on v1

--- a/solution.py
+++ b/solution.py
@@ -44,11 +44,11 @@
 
 
 def kernel(
-    slot_s, len_s, table, ql, qr, lat_hbm, rope_hbm,
+    slot_hbm, len_hbm, table_hbm, ql_hbm, qr_hbm, lat_hbm, rope_hbm,
     ctx_out, log_out,
-    lat_v, rope_v, rope_f, tab_p, tab_r, idx_v, idx_s,
+    slot_s, len_s, table, ql, qr, lat_v, rope_v, rope_f, tab_p, tab_r, idx_v, idx_s,
     stage_l, stage_r, kv, kr, krx, qs, qcat, s_ref, p_ref,
-    acc, st, r0_acc, r0_st, h_acc, h_st, r1_acc, r1_st, fin, zbuf,
+    acc, r0_acc, h_acc, h_st, r1_acc, r1_st, z_out, z_stat, z_in, z_stats, zt, zt_t,
     load_sem, idx_sem, kv_send, kv_recv, kr_send, kr_recv,
     q_send, q_recv, f_send, f_recv, r0_send, r0_recv, r1_send, r1_recv, z_send, z_recv,
 ):
@@ -90,16 +90,24 @@
     def around(steps):
         return (pool, lax.rem(z + steps, RING) * 2 + core)
 
-    load_l = pltpu.make_async_copy(lat_hbm, lat_v, load_sem.at[0])
-    load_r = pltpu.make_async_copy(rope_hbm, rope_v, load_sem.at[1])
-    load_r.start()
-    load_l.start()
+    loads = [
+        pltpu.make_async_copy(source, target, load_sem.at[i])
+        for i, (source, target) in enumerate((
+            (slot_hbm, slot_s), (len_hbm, len_s), (table_hbm, table), (ql_hbm, ql),
+            (qr_hbm, qr), (rope_hbm, rope_v), (lat_hbm, lat_v),
+        ))
+    ]
+    for copy in loads:
+        copy.start()
 
     barrier = pltpu.get_barrier_semaphore()
     greet = [peer(axis, steps) for axis in (0, 1) for steps in (1, 2, 3)]
     greet += [sibling] + [around(steps) for steps in range(1, RING)]
     for device in greet:
         pl.semaphore_signal(barrier, inc=1, device_id=device, device_id_type=MESH)
+
+    for copy in loads[0:3]:
+        copy.wait()
 
     device = pool * 32 + member
     for g in range(16):
@@ -147,6 +155,8 @@
         r = iota(shape, 0)
         return r // HALF, (r // 8) % RING, (r // 2) % 4, r % 2
 
+    for copy in loads[3:5]:
+        copy.wait()
     c_, z_, q_, h_ = parts((ROWS, ROWS))
     perm = (iota((ROWS, ROWS), 1) == q_ * 64 + 4 * z_ + 2 * c_ + h_).astype(jnp.bfloat16)
     qcat[0, :, 0:LAT] = dot(perm, ql[...]).astype(jnp.bfloat16)
@@ -161,13 +171,13 @@
         iota((ROWS, 128), 1) // 64 == h_, pair, swapped
     ).astype(jnp.bfloat16)
 
-    load_r.wait()
+    loads[5].wait()
     for i in range(32):
         rope_f[PAGES * i : PAGES * i + PAGES, :] = rope_v[:, 128 * i : 128 * i + 128].astype(
             jnp.float32
         )
     to_smem.wait()
-    load_l.wait()
+    loads[6].wait()
 
     def take(group, j):
         slot = idx_s[group, j]
@@ -190,6 +200,22 @@
         query[place].start()
 
     sent = {}
+    passed = {}
+
+    def pass_queries():
+        for place in (2, 3, 1):
+            query[place].wait_recv()
+            passed[place] = pltpu.make_async_remote_copy(
+                src_ref=qcat.at[place, half],
+                dst_ref=qcat.at[place, half],
+                send_sem=f_send.at[place],
+                recv_sem=f_recv.at[place],
+                device_id=sibling,
+                device_id_type=MESH,
+            )
+            passed[place].start()
+
+    issued = []
     for i, (axis, steps, place) in enumerate(SENDS):
         tx, ty = shift(px, py, mine[axis], steps)
         group = group_at(tx, ty, place)
@@ -216,28 +242,22 @@
                 device_id_type=MESH,
             ),
         )
-        for copy in pair_of:
-            copy.start()
+        issued.append(pair_of)
         sent[place, source] = pair_of
-
+        if i < 6:
+            for copy in pair_of:
+                copy.start()
     for a in range(4):
         for j in range(CAP):
             latent, rope = take(groups[a], j)
             kv[a, j, 0] = latent
             kr[a, j, 0] = rope
-
-    passed = {}
-    for place in (2, 3, 1):
-        query[place].wait_recv()
-        passed[place] = pltpu.make_async_remote_copy(
-            src_ref=qcat.at[place, half],
-            dst_ref=qcat.at[place, half],
-            send_sem=f_send.at[place],
-            recv_sem=f_recv.at[place],
-            device_id=sibling,
-            device_id_type=MESH,
-        )
-        passed[place].start()
+    pass_queries()
+    for i in range(6):
+        for copy in issued[i]:
+            copy.wait_send()
+        for copy in issued[i + 6]:
+            copy.start()
 
     factor = (QK_NOPE + ROPE) ** (-0.5)
     expand = (iota((256, 128), 0) // 2 == iota((256, 128), 1)).astype(jnp.bfloat16)
@@ -264,8 +284,8 @@
             p_ref[rows, :] = p
             total = jnp.sum(p.astype(jnp.float32), axis=1, keepdims=True)
             l64 = iota((64, 128), 1)
-            st[a, rows, :] = jnp.where(l64 == 0, top, jnp.where(l64 == 1, total, 0.0))
-        acc[a] = dot(p_ref[...], kv[a].reshape(SPAN, LAT))
+            acc[a, rows, LAT:] = jnp.where(l64 == 0, top, jnp.where(l64 == 1, total, 0.0))
+        acc[a, :, 0:LAT] = dot(p_ref[...], kv[a].reshape(SPAN, LAT))
 
     def merge(parts_):
         top = functools.reduce(jnp.maximum, [t for _, t, _ in parts_])
@@ -277,62 +297,51 @@
     exchange, returned = {}, {}
 
     def swap(a):
-        exchange[a] = (
-            pltpu.make_async_remote_copy(
-                src_ref=acc.at[a, rest],
-                dst_ref=r0_acc.at[a],
-                send_sem=r0_send.at[a, 0],
-                recv_sem=r0_recv.at[a, 0],
-                device_id=sibling,
-                device_id_type=MESH,
-            ),
-            pltpu.make_async_remote_copy(
-                src_ref=st.at[a, rest],
-                dst_ref=r0_st.at[a],
-                send_sem=r0_send.at[a, 1],
-                recv_sem=r0_recv.at[a, 1],
-                device_id=sibling,
-                device_id_type=MESH,
-            ),
+        exchange[a] = pltpu.make_async_remote_copy(
+            src_ref=acc.at[a, rest],
+            dst_ref=r0_acc.at[a],
+            send_sem=r0_send.at[a],
+            recv_sem=r0_recv.at[a],
+            device_id=sibling,
+            device_id_type=MESH,
         )
-        for copy in exchange[a]:
-            copy.start()
+        exchange[a].start()
 
     def halves(a):
-        for copy in exchange[a]:
-            copy.wait_recv()
-        own = st[a, half, :]
-        other = r0_st[a]
+        exchange[a].wait_recv()
+        own = acc[a, half, LAT:]
+        other = r0_acc[a, :, LAT:]
         return [
-            (acc[a, half, :], own[:, 0:1], own[:, 1:2]),
-            (r0_acc[a], other[:, 0:1], other[:, 1:2]),
+            (acc[a, half, 0:LAT], own[:, 0:1], own[:, 1:2]),
+            (r0_acc[a, :, 0:LAT], other[:, 0:1], other[:, 1:2]),
         ]
 
+    def encode(part):
+        sums, top, total = part
+        big = jnp.maximum(jnp.max(jnp.abs(sums), axis=1, keepdims=True), 1e-30)
+        steps = jnp.round(sums * (32767.0 / big)).astype(jnp.int32)
+        stats = jnp.where(
+            lane == 0, top, jnp.where(lane == 1, total, jnp.where(lane == 2, big / 32767.0, 0.0))
+        )
+        return steps, stats.T
+
     def give_back(a):
-        sums, top, total = merge(halves(a))
-        h_acc[a - 1] = sums
-        stats = jnp.where(lane == 0, top, jnp.where(lane == 1, total, 0.0))
-        h_st[a - 1] = stats.T[0:8, :]
+        steps_of, stats = encode(merge(halves(a)))
+        h_acc[a - 1] = steps_of.astype(jnp.int16)
+        h_st[a - 1] = stats[0:8, :]
         axis, steps = {1: (0, 2), 2: (1, 1), 3: (1, 3)}[a]
         slot = {1: 1, 2: 2, 3: 0}[a]
-        returned[a] = (
+        returned[a] = [
             pltpu.make_async_remote_copy(
-                src_ref=h_acc.at[a - 1],
-                dst_ref=r1_acc.at[slot],
-                send_sem=r1_send.at[slot, 0],
-                recv_sem=r1_recv.at[slot, 0],
+                src_ref=source.at[a - 1],
+                dst_ref=target.at[slot],
+                send_sem=r1_send.at[slot, k],
+                recv_sem=r1_recv.at[slot, k],
                 device_id=peer(axis, steps),
                 device_id_type=MESH,
-            ),
-            pltpu.make_async_remote_copy(
-                src_ref=h_st.at[a - 1],
-                dst_ref=r1_st.at[slot],
-                send_sem=r1_send.at[slot, 1],
-                recv_sem=r1_recv.at[slot, 1],
-                device_id=peer(axis, steps),
-                device_id_type=MESH,
-            ),
-        )
+            )
+            for k, (source, target) in enumerate(((h_st, r1_st), (h_acc, r1_acc)))
+        ]
         for copy in returned[a]:
             copy.start()
 
@@ -355,62 +364,90 @@
             copy.wait_recv()
     for slot in range(3):
         back = jnp.concatenate([r1_st[slot], jnp.zeros((120, 128), jnp.float32)], axis=0).T
-        pieces.append((r1_acc[slot], back[:, 0:1], back[:, 1:2]))
-    sums, top, total = merge(pieces)
-    fin[:, 0:LAT] = sums
-    fin[:, LAT:] = jnp.where(lane == 0, top, jnp.where(lane == 1, total, 0.0))
+        values = r1_acc[slot].astype(jnp.int32).astype(jnp.float32) * back[:, 2:3]
+        pieces.append((values, back[:, 0:1], back[:, 1:2]))
+    steps_of, stats = encode(merge(pieces))
+    blocks = steps_of.reshape(RING, 8, LAT)
+    z_out[...] = jnp.concatenate([blocks[:, :, 0:256], blocks[:, :, 256:512]], axis=1).astype(
+        jnp.int16
+    )
+    for k in range(3):
+        z_stat[k] = stats[k : k + 1, :]
 
     spread = []
     for steps in range(1, RING):
-        rows = pl.ds(pl.multiple_of(lax.rem(z + steps, RING) * 8, 8), 8)
-        copy = pltpu.make_async_remote_copy(
-            src_ref=fin.at[rows],
-            dst_ref=zbuf.at[steps],
-            send_sem=z_send.at[steps],
-            recv_sem=z_recv.at[steps],
-            device_id=around(steps),
-            device_id_type=MESH,
-        )
-        copy.start()
-        spread.append(copy)
-    zbuf[0] = fin[pl.ds(pl.multiple_of(z * 8, 8), 8), :]
-    for copy in spread:
-        copy.wait_recv()
-    pieces = [
-        (zbuf[i, :, 0:LAT], zbuf[i, :, LAT : LAT + 1], zbuf[i, :, LAT + 1 : LAT + 2])
-        for i in range(RING)
-    ]
-    sums, top, total = merge(pieces)
-    ctx_out[...] = sums / total
+        spread.append([
+            pltpu.make_async_remote_copy(
+                src_ref=source,
+                dst_ref=target.at[steps],
+                send_sem=z_send.at[steps, k],
+                recv_sem=z_recv.at[steps, k],
+                device_id=around(steps),
+                device_id_type=MESH,
+            )
+            for k, (source, target) in enumerate((
+                (z_stat, z_stats), (z_out.at[lax.rem(z + steps, RING)], z_in),
+            ))
+        ])
+    for k in range(2):
+        for copies in spread:
+            copies[k].start()
+    z_in[0] = z_out[z]
+    z_stats[0] = z_stat[...]
+    zt[...] = jnp.zeros((128, 128), jnp.float32)
+    for i in range(RING):
+        if i:
+            spread[i - 1][0].wait_recv()
+        for k in range(3):
+            zt[16 * k + i : 16 * k + i + 1, :] = z_stats[i, k]
+    zt_t[...] = zt[...].T
+    mine_t = zt_t[pl.ds(pl.multiple_of(z * 8, 8), 8), :]
+    tops = mine_t[:, 0:16]
+    top = jnp.max(tops, axis=1, keepdims=True)
+    weight = jnp.exp(tops - top)
+    total = jnp.sum(weight * mine_t[:, 16:32], axis=1, keepdims=True)
+    weight = weight * mine_t[:, 32:48] / total
+    weight = jnp.concatenate([weight, weight], axis=0)
     log_out[...] = jnp.broadcast_to(top + jnp.log(total), (8, 128))
-
-    for copy in spread:
-        copy.wait_send()
+    context = jnp.zeros((16, 256), jnp.float32)
+    for i in range(RING):
+        if i:
+            spread[i - 1][1].wait_recv()
+        context += z_in[i].astype(jnp.int32).astype(jnp.float32) * weight[:, i : i + 1]
+    ctx_out[:, 0:256] = context[0:8]
+    ctx_out[:, 256:512] = context[8:16]
+
+    for copies in spread:
+        for copy in copies:
+            copy.wait_send()
     for place in (1, 2, 3):
         query[place].wait_send()
         passed[place].wait_send()
         for copy in returned[place]:
             copy.wait_send()
     for a in range(4):
-        for copy in exchange[a]:
-            copy.wait_send()
-    for pair_of in sent.values():
+        exchange[a].wait_send()
+    for pair_of in issued[6:]:
         for copy in pair_of:
             copy.wait_send()
 
 
 def per_device(q_latent, q_rope, pool_latent, pool_rope, page_table, lengths, slot_request):
     vmem = pl.BlockSpec(memory_space=pltpu.VMEM)
-    smem = pl.BlockSpec(memory_space=pltpu.SMEM)
     anywhere = pl.BlockSpec(memory_space=pl.ANY)
-    f32, bf16, i32 = jnp.float32, jnp.bfloat16, jnp.int32
+    f32, bf16, i32, i16 = jnp.float32, jnp.bfloat16, jnp.int32, jnp.int16
     dma = pltpu.SemaphoreType.DMA
     ctx, log = pl.pallas_call(
         kernel,
         out_shape=(jax.ShapeDtypeStruct((8, LAT), f32), jax.ShapeDtypeStruct((8, 128), f32)),
-        in_specs=[smem, smem, vmem, vmem, vmem, anywhere, anywhere],
+        in_specs=[anywhere] * 7,
         out_specs=(vmem, vmem),
         scratch_shapes=[
+            pltpu.SMEM((16,), i32),
+            pltpu.SMEM((16,), i32),
+            pltpu.VMEM((16, MAXP), i32),
+            pltpu.VMEM((ROWS, LAT), bf16),
+            pltpu.VMEM((4, 64 * ROPE), bf16),
             pltpu.VMEM((PAGES, TOK, LAT), bf16),
             pltpu.VMEM((PAGES, TOK * ROPE), bf16),
             pltpu.VMEM((32 * PAGES, 128), f32),
@@ -427,17 +464,19 @@
             pltpu.VMEM((4, ROWS, LAT + 128), bf16),
             pltpu.VMEM((ROWS, SPAN), f32),
             pltpu.VMEM((ROWS, SPAN), bf16),
-            pltpu.VMEM((4, ROWS, LAT), f32),
-            pltpu.VMEM((4, ROWS, 128), f32),
-            pltpu.VMEM((4, HALF, LAT), f32),
-            pltpu.VMEM((4, HALF, 128), f32),
-            pltpu.VMEM((3, HALF, LAT), f32),
+            pltpu.VMEM((4, ROWS, LAT + 128), f32),
+            pltpu.VMEM((4, HALF, LAT + 128), f32),
+            pltpu.VMEM((3, HALF, LAT), i16),
             pltpu.VMEM((3, 8, 128), f32),
-            pltpu.VMEM((3, HALF, LAT), f32),
+            pltpu.VMEM((3, HALF, LAT), i16),
             pltpu.VMEM((3, 8, 128), f32),
-            pltpu.VMEM((HALF, LAT + 128), f32),
-            pltpu.VMEM((RING, 8, LAT + 128), f32),
-            dma((2,)),
+            pltpu.VMEM((RING, 16, 256), i16),
+            pltpu.VMEM((3, 1, 128), f32),
+            pltpu.VMEM((RING, 16, 256), i16),
+            pltpu.VMEM((RING, 3, 1, 128), f32),
+            pltpu.VMEM((128, 128), f32),
+            pltpu.VMEM((128, 128), f32),
+            dma((7,)),
             dma,
             dma((12,)),
             dma((4, 4)),
@@ -447,15 +486,15 @@
             dma((4,)),
             dma((4,)),
             dma((4,)),
-            dma((4, 2)),
-            dma((4, 2)),
+            dma((4,)),
+            dma((4,)),
             dma((3, 2)),
             dma((3, 2)),
-            dma((RING,)),
-            dma((RING,)),
+            dma((RING, 2)),
+            dma((RING, 2)),
         ],
         compiler_params=pltpu.CompilerParams(
-            collective_id=0, has_side_effects=True, vmem_limit_bytes=48 * 2**20
+            collective_id=0, has_side_effects=True, vmem_limit_bytes=60 * 2**20
         ),
         cost_estimate=pl.CostEstimate(flops=2 * 10**9, bytes_accessed=4 * 10**6, transcendentals=10**6),
     )(

time: 83.1 us -> 65.6 us (0.79)
  the two profiles are of different devices: /device:TPU:10 before, /device:TPU:16 now
where the time goes in v2:
time: 65.6 us; the launch traced here: 65.4 us
  Pallas kernels  61.9 us (94%)
  local copies, waits for them, and re-layouts  2.14 us (3%)
  other arithmetic  0.72 us (1%)
    pallas_call x1, Pallas kernels, per_device(): pl.pallas_call(kernel, out_shape=(jax.ShapeDtypeStruct((8, LAT), f32), ja...  61.9 us

profile of v2, /device:TPU:16, one launch (start us, length us, event | category | flops | bytes accessed | tf_op | source)
XLA Modules:
  0.0 65.4 jit_solution(1838015803586276141)
XLA Ops:
  0.6 61.9 %shard_map.86 = (f32[8,512]{1,0:T(8,128)}, f32[8,128]{1,0:T(8,128)}) custom-call(s32[16]{0:T(128)} %slot_hbm.1, s32[16]{0:T(128)} %len_hbm.1, s32[16,1536]{1,0:T(8,128)} %table_hbm.1, bf16[256,512]{1,0:T(8,128)(2,1)} %bitcast.2, bf16[4,4096]{1,0:T(4,128)(2,1)} %bitcast.3, bf16[48,64,512]{2,1,0:T(8,128)(2,1)} %lat_hbm.1, bf16[48,4096]{1,0:T(8,128)(2,1)} %rope_hbm.1), custom_call_target="tpu_custom_call" | custom-call | flops 2000000000 | bytes 4000000 | tf_op jit(solution)/shard_map/pallas_call | solution.py:440
  62.5 0.7 %convert_element_type.3 = bf16[8,512]{1,0:T(8,128)(2,1)S(1)} convert(f32[8,512]{1,0:T(8,128)} %get-tuple-element.4) | non-fusion elementwise | flops 4096 | bytes 24576 | tf_op jit(solution)/shard_map/convert_element_type | solution.py:509
  63.2 0.6 reshape.15
  63.9 0.8 %slice_reduce_fusion = f32[8]{0:T(128)S(1)} fusion(f32[8,128]{1,0:T(8,128)} %get-tuple-element.5), kind=kLoop, calls=%fused_computation | loop fusion | bytes 64 | tf_op jit(solution)/shard_map/slice | solution.py:510
  64.6 0.1 reshape_squeeze.3
  64.7 0.7 %copy.10 = f32[1,4,2]{1,2,0:T(2,128)} copy(f32[1,4,2]{2,1,0:T(4,128)S(1)} %reshape_squeeze.3) | data formatting | bytes 64

commit v3 on v2

v3 whole, which is shorter than its diff:
```python
import functools

import jax
import jax.numpy as jnp
from jax import lax
from jax.experimental import pallas as pl
from jax.experimental.pallas import tpu as pltpu
from jax.sharding import PartitionSpec as P

MESH = pl.DeviceIdType.MESH
QK_NOPE = 128
NEG = -1e30
EMPTY = -1e29

SIDE = 4
RING = 16
PAGES = 48
CAP = 3
TOK = 64
LAT = 512
ROPE = 64
ROWS = 256
PART = 64
SPAN = 768
MAXP = 1536

SENDS = (
    (1, 2, 1), (1, 1, 2), (1, 3, 2), (0, 2, 2), (0, 1, 1), (0, 3, 1),
    (1, 1, 3), (1, 3, 3), (0, 2, 3),
    (1, 2, 0), (0, 1, 0), (0, 3, 0),
)
FAR = (8, 7, 9, 6, 10, 5, 11, 4)
NEAR = (12, 3, 13, 2, 14, 1, 15)


def dot(a, b):
    return jnp.dot(a, b, preferred_element_type=jnp.float32)


def dot_t(a, b):
    return lax.dot_general(a, b, (((1,), (1,)), ((), ())), preferred_element_type=jnp.float32)


def iota(shape, dim):
    return lax.broadcasted_iota(jnp.int32, shape, dim)


def kernel(
    slot_hbm, len_hbm, table_hbm, ql_hbm, qr_hbm, lat_hbm, rope_hbm,
    out,
    slot_s, len_s, table, ql, qr, lat_v, rope_v, rope_f, tab_p, tab_r, idx_v, idx_s,
    stage_l, stage_r, kv, kr, krx, qs, qcat, s_ref, p_ref,
    acc, r0_acc, h_acc, h_st, r1_acc, r1_st, z_out, z_stat, z_in, z_stats, zt,
    load_sem, idx_sem, kv_send, kv_recv, kr_send, kr_recv,
    q_send, q_recv, f_send, f_recv, r0_send, r0_recv, r1_send, r1_recv, z_send, z_recv,
):
    pool = lax.axis_index("pool")
    member = lax.axis_index("dcp")
    px, py = pool // SIDE, pool % SIDE
    z, core = member // 2, member % 2

    def wait(ref, sem):
        pltpu.make_async_copy(ref, ref, sem).wait()

    def wrap(v):
        return lax.rem(v + 2 * SIDE, SIDE)

    def axes(x, y):
        odd = lax.rem(x + y, 2)
        return ((odd, 1 - odd), (1 - odd, odd))

    def shift(x, y, unit, steps):
        return wrap(x + steps * unit[0]), wrap(y + steps * unit[1])

    def group_at(x, y, place):
        other, key = axes(x, y)
        if place == 0:
            gx, gy = x, y
        elif place == 1:
            gx, gy = shift(x, y, other, 2)
        elif place == 2:
            gx, gy = shift(x, y, key, 1)
        else:
            gx, gy = shift(x, y, key, 3)
        return gx * SIDE + gy

    mine = axes(px, py)

    def peer(axis, steps):
        x, y = shift(px, py, mine[axis], steps)
        return (x * SIDE + y, member)

    sibling = (pool, z * 2 + 1 - core)

    def around(steps):
        return (pool, lax.rem(z + steps, RING) * 2 + core)

    loads = [
        pltpu.make_async_copy(source, target, load_sem.at[i])
        for i, (source, target) in enumerate((
            (slot_hbm, slot_s), (len_hbm, len_s), (table_hbm, table), (ql_hbm, ql),
            (qr_hbm, qr), (rope_hbm, rope_v), (lat_hbm, lat_v),
        ))
    ]
    for copy in loads:
        copy.start()

    barrier = pltpu.get_barrier_semaphore()
    greet = [peer(axis, steps) for axis in (0, 1) for steps in (1, 2, 3)]
    greet += [sibling] + [around(steps) for steps in range(1, RING)]
    for device in greet:
        pl.semaphore_signal(barrier, inc=1, device_id=device, device_id_type=MESH)

    for copy in loads[0:3]:
        copy.wait()

    device = pool * 32 + member
    for g in range(16):
        tab_p[pl.ds(g, 1), :] = table[pl.ds(slot_s[g], 1), :] - device * PAGES
    groups = [group_at(px, py, a) for a in range(4)]
    for a in range(4):
        row = table[pl.ds(slot_s[groups[a]], 1), :]
        for b in range(4):
            x, y = shift(px, py, mine[1] if a < 2 else mine[0], b)
            tab_r[pl.ds(4 * a + b, 1), :] = row - ((x * SIDE + y) * 32 + member) * PAGES

    def picks(tab):
        local = jnp.where((tab >= 0) & (tab < PAGES), tab, 64)
        found = []
        for _ in range(CAP):
            first = jnp.min(local, axis=1, keepdims=True)
            found.append(first)
            local = jnp.where(local > first, local, 64)
        return found

    def lanes(values):
        lane = iota((16, 128), 1)
        out = jnp.zeros((16, 128), jnp.int32)
        for j in range(CAP):
            out = jnp.where(lane == j, values[j], out)
        return out

    idx_v[0:16, :] = lanes([jnp.minimum(v, PAGES - 1) for v in picks(tab_p[...])])
    tab = tab_r[...]
    page = iota((16, MAXP), 1)
    quarter = iota((16, 1), 0) // 4
    length = jnp.zeros((16, 1), jnp.int32)
    for a in range(4):
        length = jnp.where(quarter == a, len_s[slot_s[groups[a]]], length)
    counts = []
    for first in picks(tab):
        number = jnp.sum(jnp.where(tab == first, page, 0), axis=1, keepdims=True)
        count = jnp.clip(length - number * TOK, 0, TOK)
        counts.append(jnp.where(first < 64, count, 0))
    idx_v[16:32, :] = lanes(counts)
    to_smem = pltpu.make_async_copy(idx_v, idx_s, idx_sem)
    to_smem.start()

    def parts(shape):
        r = iota(shape, 0)
        steps = (r // 128) * 8 + 4 + (r // 8) % 8
        return (r // PART) % 2, (z + steps) % RING, (r // 2) % 4, r % 2

    for copy in loads[3:5]:
        copy.wait()
    c_, z_, q_, h_ = parts((ROWS, ROWS))
    perm = (iota((ROWS, ROWS), 1) == q_ * 64 + 4 * z_ + 2 * c_ + h_).astype(jnp.bfloat16)

    def split(rows):
        return rows.astype(jnp.bfloat16).reshape(2, 2, PART, -1)

    qcat[0, :, :, :, 0:LAT] = split(dot(perm, ql[...]))
    rope_rows = qr[...].astype(jnp.float32)
    for i in range(32):
        qs[4 * i : 4 * i + 4, :] = rope_rows[:, 128 * i : 128 * i + 128]
    c_, z_, q_, h_ = parts((ROWS, 128))
    pick = (iota((ROWS, 128), 1) == (2 * z_ + c_) * 4 + q_).astype(jnp.bfloat16)
    pair = dot(pick, qs[...].astype(jnp.bfloat16))
    swapped = jnp.concatenate([pair[:, 64:128], pair[:, 0:64]], axis=1)
    qcat[0, :, :, :, LAT:] = split(jnp.where(iota((ROWS, 128), 1) // 64 == h_, pair, swapped))

    to_smem.wait()
    pl.semaphore_wait(barrier, len(greet))

    query = {}
    for steps, place in ((1, 3), (3, 2), (2, 1)):
        query[place] = pltpu.make_async_remote_copy(
            src_ref=qcat.at[0, :, core],
            dst_ref=qcat.at[place, :, core],
            send_sem=q_send,
            recv_sem=q_recv.at[place],
            device_id=peer(0, steps),
            device_id_type=MESH,
        )
        query[place].start()

    loads[5].wait()
    for i in range(32):
        rope_f[PAGES * i : PAGES * i + PAGES, :] = rope_v[:, 128 * i : 128 * i + 128].astype(
            jnp.float32
        )
    loads[6].wait()

    def take(group, j):
        slot = idx_s[group, j]
        return lat_v[slot], rope_f[pl.ds(slot, 32, stride=PAGES), :].astype(jnp.bfloat16)

    passed = {}

    def pass_queries():
        for place in (2, 3, 1):
            query[place].wait_recv()
            passed[place] = pltpu.make_async_remote_copy(
                src_ref=qcat.at[place, :, core],
                dst_ref=qcat.at[place, :, core],
                send_sem=f_send,
                recv_sem=f_recv.at[place],
                device_id=sibling,
                device_id_type=MESH,
            )
            passed[place].start()

    def pack(i):
        axis, steps, place = SENDS[i]
        group = group_at(*shift(px, py, mine[axis], steps), place)
        for j in range(CAP):
            latent, rope = take(group, j)
            stage_l[i, j] = latent
            stage_r[i, j] = rope

    def send(i):
        axis, steps, place = SENDS[i]
        for source, target, sends, recvs in (
            (stage_l, kv, kv_send, kv_recv), (stage_r, kr, kr_send, kr_recv),
        ):
            pltpu.make_async_remote_copy(
                src_ref=source.at[i],
                dst_ref=target.at[place, :, 4 - steps],
                send_sem=sends,
                recv_sem=recvs.at[place],
                device_id=peer(axis, steps),
                device_id_type=MESH,
            ).start()

    for i in range(12):
        pack(i)
        send(i)
    pass_queries()
    for a in range(4):
        for j in range(CAP):
            latent, rope = take(groups[a], j)
            kv[a, j, 0] = latent
            kr[a, j, 0] = rope

    factor = (QK_NOPE + ROPE) ** (-0.5)
    expand = (iota((256, 128), 0) // 2 == iota((256, 128), 1)).astype(jnp.bfloat16)
    parity = iota((256, 128), 1) // 64 == iota((256, 128), 0) % 2
    within = iota((1, 256), 1) % TOK
    source_of = iota((1, 256), 1) // TOK
    lane = iota((128, 128), 1)

    def expand_keys(a):
        for j in range(CAP):
            pairs = kr[a, j].reshape(128, 128)
            krx[a, 256 * j : 256 * j + 256, :] = jnp.where(
                parity, dot(expand, pairs), 0.0
            ).astype(jnp.bfloat16)

    def attend(a, k):
        rows_l = qcat[a, k, :, :, 0:LAT].reshape(128, LAT)
        rows_r = qcat[a, k, :, :, LAT:].reshape(128, 128)
        for j in range(CAP):
            keys = kv[a, j].reshape(256, LAT)
            scores = dot_t(rows_l, keys) + dot_t(rows_r, krx[a, 256 * j : 256 * j + 256, :])
            limit = jnp.zeros((1, 256), jnp.int32)
            for b in range(4):
                limit = jnp.where(source_of == b, idx_s[16 + 4 * a + b, j], limit)
            s_ref[:, 256 * j : 256 * j + 256] = jnp.where(within < limit, scores * factor, NEG)
        for c in range(2):
            rows = slice(PART * c, PART * c + PART)
            s = s_ref[rows, :]
            top = jnp.maximum(jnp.max(s, axis=1, keepdims=True), EMPTY)
            p = jnp.exp(s - top).astype(jnp.bfloat16)
            p_ref[rows, :] = p
            total = jnp.sum(p.astype(jnp.float32), axis=1, keepdims=True)
            acc[a, k, c, :, LAT:] = jnp.where(
                lane[0:PART] == 0, top, jnp.where(lane[0:PART] == 1, total, 0.0)
            )
        acc[a, k, :, :, 0:LAT] = dot(p_ref[...], kv[a].reshape(SPAN, LAT)).reshape(2, PART, LAT)

    def merge(parts_):
        top = functools.reduce(jnp.maximum, [t for _, t, _ in parts_])
        scales = [jnp.exp(t - top) for _, t, _ in parts_]
        total = sum(w * l for w, (_, _, l) in zip(scales, parts_))
        sums = sum(w * v for w, (v, _, _) in zip(scales, parts_))
        return sums, top, total

    exchange = {}

    def swap(a, k):
        exchange[a, k] = pltpu.make_async_remote_copy(
            src_ref=acc.at[a, k, 1 - core],
            dst_ref=r0_acc.at[a, k],
            send_sem=r0_send,
            recv_sem=r0_recv.at[a, k],
            device_id=sibling,
            device_id_type=MESH,
        )
        exchange[a, k].start()

    def halves(a, k):
        exchange[a, k].wait_recv()
        own = acc[a, k, core]
        other = r0_acc[a, k]
        return [(v[:, 0:LAT], v[:, LAT : LAT + 1], v[:, LAT + 1 : LAT + 2]) for v in (own, other)]

    def encode(part):
        sums, top, total = part
        big = jnp.maximum(jnp.max(jnp.abs(sums), axis=1, keepdims=True), 1e-30)
        steps = jnp.round(sums * (32767.0 / big)).astype(jnp.int32)
        first = jnp.concatenate([top, total], axis=0)
        second = jnp.concatenate([big / 32767.0, big], axis=0)
        stats = jnp.where(lane == 0, first, jnp.where(lane == 1, second, 0.0)).T
        return steps, stats

    def give_back(a, k):
        steps_of, stats = encode(merge(halves(a, k)))
        h_acc[a - 1, k] = steps_of.astype(jnp.int16)
        h_st[a - 1, k] = stats[0:8, :]
        axis, steps = {1: (0, 2), 2: (1, 1), 3: (1, 3)}[a]
        slot = {1: 1, 2: 2, 3: 0}[a]
        for n, (source, target) in enumerate(((h_st, r1_st), (h_acc, r1_acc))):
            pltpu.make_async_remote_copy(
                src_ref=source.at[a - 1, k],
                dst_ref=target.at[k, slot],
                send_sem=r1_send.at[n],
                recv_sem=r1_recv.at[k, n],
                device_id=peer(axis, steps),
                device_id_type=MESH,
            ).start()

    def finish(k):
        pieces = halves(0, k)
        for n, target in enumerate((r1_st, r1_acc)):
            wait(target.at[k], r1_recv.at[k, n])
        for slot in range(3):
            back = jnp.concatenate([r1_st[k, slot], jnp.zeros((120, 128), jnp.float32)], axis=0).T
            values = r1_acc[k, slot].astype(jnp.int32).astype(jnp.float32) * back[0:PART, 1:2]
            pieces.append((values, back[0:PART, 0:1], back[PART:, 0:1]))
        steps_of, stats = encode(merge(pieces))
        blocks = steps_of.reshape(8, 8, LAT)
        z_out[k] = jnp.concatenate([blocks[:, :, 0:256], blocks[:, :, 256:512]], axis=1).astype(
            jnp.int16
        )
        for n in range(2):
            z_stat[k, n] = stats[n : n + 1, :]
        for n in range(2):
            for steps in (FAR, NEAR)[k]:
                copy = pltpu.make_async_remote_copy(
                    src_ref=(z_stat.at[k], z_out.at[k, (steps + 4) % 8])[n],
                    dst_ref=(z_stats, z_in)[n].at[steps],
                    send_sem=z_send.at[n],
                    recv_sem=z_recv.at[n],
                    device_id=around(steps),
                    device_id_type=MESH,
                )
                copy.start()

    for a in (1, 2, 3, 0):
        if a:
            passed[a].wait_recv()
        wait(kv.at[a, :, 1:4], kv_recv.at[a])
        wait(kr.at[a, :, 1:4], kr_recv.at[a])
        expand_keys(a)
        for k in range(2):
            attend(a, k)
            swap(a, k)
        if a:
            give_back(a, 0)
            give_back(a, 1)
    finish(0)
    finish(1)

    z_in[0] = z_out[1, 4]
    z_stats[0] = z_stat[1]
    zt[...] = jnp.zeros((128, 128), jnp.float32)
    wait(z_stats.at[1:RING], z_recv.at[0])
    for i in range(RING):
        for n in range(2):
            zt[16 * n + i : 16 * n + i + 1, :] = z_stats[i, n]
    turned = zt[...].T
    which = (iota((8, 128), 1) % 16 + 4) % 8
    tops = jnp.zeros((8, 128), jnp.float32)
    totals = tops
    for j in range(8):
        tops = jnp.where(which == j, turned[8 * j : 8 * j + 8], tops)
        totals = jnp.where(which == j, turned[PART + 8 * j : PART + 8 * j + 8], totals)
    sizes, tops, totals = tops[:, 16:32], tops[:, 0:16], totals[:, 0:16]
    top = jnp.max(tops, axis=1, keepdims=True)
    weight = jnp.exp(tops - top)
    total = jnp.sum(weight * totals, axis=1, keepdims=True)
    weight = weight * sizes / total
    weight = jnp.concatenate([weight, weight], axis=0)
    context = jnp.zeros((16, 256), jnp.float32)
    wait(z_in.at[1:RING], z_recv.at[1])
    for i in range(RING):
        context += z_in[i].astype(jnp.int32).astype(jnp.float32) * weight[:, i : i + 1]
    out[:, 0:256] = context[0:8]
    out[:, 256:512] = context[8:16]
    out[:, 512:] = jnp.broadcast_to(top + jnp.log(total), (8, 128))

    wait(z_stats.at[1:RING], z_send.at[0])
    wait(z_in.at[1:RING], z_send.at[1])
    wait(qcat.at[1:4, :, 0], q_send)
    wait(qcat.at[1:4, :, 0], f_send)
    wait(stage_l, kv_send)
    wait(stage_r, kr_send)
    wait(r0_acc, r0_send)
    wait(h_st, r1_send.at[0])
    wait(h_acc, r1_send.at[1])


def layout_kernel(rows, ctx_out, log_out):
    for q in range(4):
        ctx_out[q] = rows[2 * q : 2 * q + 2, 0:LAT].astype(jnp.bfloat16)
    cell, spot = iota((8, 128), 0), iota((8, 128), 1)
    for h in range(2):
        line = jnp.where((cell % 2 == h) & (spot == cell // 2), rows[:, LAT:], 0.0)
        log_out[h : h + 1, :] = jnp.sum(line, axis=0, keepdims=True)[:, 0:4]


def per_device(q_latent, q_rope, pool_latent, pool_rope, page_table, lengths, slot_request):
    vmem = pl.BlockSpec(memory_space=pltpu.VMEM)
    anywhere = pl.BlockSpec(memory_space=pl.ANY)
    f32, bf16, i32, i16 = jnp.float32, jnp.bfloat16, jnp.int32, jnp.int16
    dma = pltpu.SemaphoreType.DMA
    rows = pl.pallas_call(
        kernel,
        out_shape=jax.ShapeDtypeStruct((8, LAT + 128), f32),
        in_specs=[anywhere] * 7,
        out_specs=vmem,
        scratch_shapes=[
            pltpu.SMEM((16,), i32),
            pltpu.SMEM((16,), i32),
            pltpu.VMEM((16, MAXP), i32),
            pltpu.VMEM((ROWS, LAT), bf16),
            pltpu.VMEM((4, 64 * ROPE), bf16),
            pltpu.VMEM((PAGES, TOK, LAT), bf16),
            pltpu.VMEM((PAGES, TOK * ROPE), bf16),
            pltpu.VMEM((32 * PAGES, 128), f32),
            pltpu.VMEM((16, MAXP), i32),
            pltpu.VMEM((16, MAXP), i32),
            pltpu.VMEM((32, 128), i32),
            pltpu.SMEM((32, 128), i32),
            pltpu.VMEM((12, CAP, TOK, LAT), bf16),
            pltpu.VMEM((12, CAP, 32, 128), bf16),
            pltpu.VMEM((4, CAP, 4, TOK, LAT), bf16),
            pltpu.VMEM((4, CAP, 4, 32, 128), bf16),
            pltpu.VMEM((4, SPAN, 128), bf16),
            pltpu.VMEM((128, 128), f32),
            pltpu.VMEM((4, 2, 2, PART, LAT + 128), bf16),
            pltpu.VMEM((128, SPAN), f32),
            pltpu.VMEM((128, SPAN), bf16),
            pltpu.VMEM((4, 2, 2, PART, LAT + 128), f32),
            pltpu.VMEM((4, 2, PART, LAT + 128), f32),
            pltpu.VMEM((3, 2, PART, LAT), i16),
            pltpu.VMEM((3, 2, 8, 128), f32),
            pltpu.VMEM((2, 3, PART, LAT), i16),
            pltpu.VMEM((2, 3, 8, 128), f32),
            pltpu.VMEM((2, 8, 16, 256), i16),
            pltpu.VMEM((2, 2, 1, 128), f32),
            pltpu.VMEM((RING, 16, 256), i16),
            pltpu.VMEM((RING, 2, 1, 128), f32),
            pltpu.VMEM((128, 128), f32),
            dma((7,)),
            dma,
            dma,
            dma((4,)),
            dma,
            dma((4,)),
            dma,
            dma((4,)),
            dma,
            dma((4,)),
            dma,
            dma((4, 2)),
            dma((2,)),
            dma((2, 2)),
            dma((2,)),
            dma((2,)),
        ],
        compiler_params=pltpu.CompilerParams(
            collective_id=0, has_side_effects=True, vmem_limit_bytes=60 * 2**20
        ),
        cost_estimate=pl.CostEstimate(flops=2 * 10**9, bytes_accessed=4 * 10**6, transcendentals=10**6),
    )(
        slot_request,
        lengths,
        page_table,
        q_latent.reshape(ROWS, LAT),
        q_rope.reshape(4, 64 * ROPE),
        pool_latent,
        pool_rope,
    )
    ctx, log = pl.pallas_call(
        layout_kernel,
        out_shape=(jax.ShapeDtypeStruct((4, 2, LAT), bf16), jax.ShapeDtypeStruct((2, 4), f32)),
        in_specs=[vmem],
        out_specs=(vmem, vmem),
        compiler_params=pltpu.CompilerParams(vmem_limit_bytes=60 * 2**20),
    )(rows)
    return ctx.reshape(1, 4, 2, LAT), log.T.reshape(1, 4, 2)


def solution(mesh):
    in_specs = (
        P("pool", None, None, None),
        P("pool", None, None),
        P(("pool", "dcp"), None, None),
        P(("pool", "dcp"), None),
        P(),
        P(),
        P(),
    )
    out_specs = (P("pool", None, "dcp", None), P("pool", None, "dcp"))
    return jax.shard_map(
        per_device, mesh=mesh, in_specs=in_specs, out_specs=out_specs, check_vma=False
    )
```

time: 65.6 us -> 60.6 us (0.924)
  the two profiles are of different devices: /device:TPU:16 before, /device:TPU:1 now
where the time goes in v3:
time: 60.6 us; the launch traced here: 60.5 us
  Pallas kernels  59.8 us (99%)
  between operations  0.64 us (1%)
    pallas_call x1, Pallas kernels, per_device(): pl.pallas_call(kernel, out_shape=jax.ShapeDtypeStruct((8, LAT + 128), f32...  58.5 us
    pallas_call x1, Pallas kernels, per_device(): pl.pallas_call(layout_kernel, out_shape=(jax.ShapeDtypeStruct((4, 2, LAT)...  1.34 us

profile of v3, /device:TPU:1, one launch (start us, length us, event | category | flops | bytes accessed | tf_op | source)
XLA Modules:
  0.0 60.5 jit_solution(7642944923434993147)
XLA Ops:
  0.6 58.5 %shard_map.86.rows = f32[8,640]{1,0:T(8,128)} custom-call(s32[16]{0:T(128)} %slot_hbm.1, s32[16]{0:T(128)} %len_hbm.1, s32[16,1536]{1,0:T(8,128)} %table_hbm.1, bf16[256,512]{1,0:T(8,128)(2,1)} %bitcast.6, bf16[4,4096]{1,0:T(4,128)(2,1)} %bitcast.7, bf16[48,64,512]{2,1,0:T(8,128)(2,1)} %lat_hbm.1, bf16[48,4096]{1,0:T(8,128)(2,1)} %rope_hbm.1), custom_call_target="tpu_custom_call" | custom-call | flops 2000000000 | bytes 4000000 | tf_op jit(solution)/shard_map/pallas_call | solution.py:437
  59.1 1.3 %shard_map.87 = (bf16[4,2,512]{2,1,0:T(2,128)(2,1)}, f32[2,4]{1,0:T(2,128)}) custom-call(f32[8,640]{1,0:T(8,128)} %shard_map.86.rows), custom_call_target="tpu_custom_call" | custom-call | tf_op jit(solution)/shard_map/pallas_call | solution.py:505

commit v4 on v3

--- a/solution.py
+++ b/solution.py
@@ -25,9 +25,7 @@
 MAXP = 1536
 
 SENDS = (
-    (1, 2, 1), (1, 1, 2), (1, 3, 2), (0, 2, 2), (0, 1, 1), (0, 3, 1),
-    (1, 1, 3), (1, 3, 3), (0, 2, 3),
-    (1, 2, 0), (0, 1, 0), (0, 3, 0),
+    (1, 2, 1), (0, 2, 2), (1, 1, 2), (1, 3, 2), (0, 1, 1), (0, 3, 1), (0, 2, 3), (1, 1, 3), (1, 3, 3), (1, 2, 0), (0, 1, 0), (0, 3, 0),
 )
 FAR = (8, 7, 9, 6, 10, 5, 11, 4)
 NEAR = (12, 3, 13, 2, 14, 1, 15)
@@ -110,6 +108,43 @@
     greet += [sibling] + [around(steps) for steps in range(1, RING)]
     for device in greet:
         pl.semaphore_signal(barrier, inc=1, device_id=device, device_id_type=MESH)
+
+    def parts(shape):
+        r = iota(shape, 0)
+        steps = (r // 128) * 8 + 4 + (r // 8) % 8
+        return (r // PART) % 2, (z + steps) % RING, (r // 2) % 4, r % 2
+
+    for copy in loads[3:5]:
+        copy.wait()
+    c_, z_, q_, h_ = parts((ROWS, ROWS))
+    perm = (iota((ROWS, ROWS), 1) == q_ * 64 + 4 * z_ + 2 * c_ + h_).astype(jnp.bfloat16)
+
+    def split(rows):
+        return rows.astype(jnp.bfloat16).reshape(2, 2, PART, -1)
+
+    qcat[0, :, :, :, 0:LAT] = split(dot(perm, ql[...]))
+    rope_rows = qr[...].astype(jnp.float32)
+    for i in range(32):
+        qs[4 * i : 4 * i + 4, :] = rope_rows[:, 128 * i : 128 * i + 128]
+    c_, z_, q_, h_ = parts((ROWS, 128))
+    pick = (iota((ROWS, 128), 1) == (2 * z_ + c_) * 4 + q_).astype(jnp.bfloat16)
+    pair = dot(pick, qs[...].astype(jnp.bfloat16))
+    swapped = jnp.concatenate([pair[:, 64:128], pair[:, 0:64]], axis=1)
+    qcat[0, :, :, :, LAT:] = split(jnp.where(iota((ROWS, 128), 1) // 64 == h_, pair, swapped))
+
+    pl.semaphore_wait(barrier, len(greet))
+
+    query = {}
+    for steps, place in ((2, 1), (1, 3), (3, 2)):
+        query[place] = pltpu.make_async_remote_copy(
+            src_ref=qcat.at[0, :, core],
+            dst_ref=qcat.at[place, :, core],
+            send_sem=q_send,
+            recv_sem=q_recv.at[place],
+            device_id=peer(0, steps),
+            device_id_type=MESH,
+        )
+        query[place].start()
 
     for copy in loads[0:3]:
         copy.wait()
@@ -156,49 +191,13 @@
     to_smem = pltpu.make_async_copy(idx_v, idx_s, idx_sem)
     to_smem.start()
 
-    def parts(shape):
-        r = iota(shape, 0)
-        steps = (r // 128) * 8 + 4 + (r // 8) % 8
-        return (r // PART) % 2, (z + steps) % RING, (r // 2) % 4, r % 2
-
-    for copy in loads[3:5]:
-        copy.wait()
-    c_, z_, q_, h_ = parts((ROWS, ROWS))
-    perm = (iota((ROWS, ROWS), 1) == q_ * 64 + 4 * z_ + 2 * c_ + h_).astype(jnp.bfloat16)
-
-    def split(rows):
-        return rows.astype(jnp.bfloat16).reshape(2, 2, PART, -1)
-
-    qcat[0, :, :, :, 0:LAT] = split(dot(perm, ql[...]))
-    rope_rows = qr[...].astype(jnp.float32)
-    for i in range(32):
-        qs[4 * i : 4 * i + 4, :] = rope_rows[:, 128 * i : 128 * i + 128]
-    c_, z_, q_, h_ = parts((ROWS, 128))
-    pick = (iota((ROWS, 128), 1) == (2 * z_ + c_) * 4 + q_).astype(jnp.bfloat16)
-    pair = dot(pick, qs[...].astype(jnp.bfloat16))
-    swapped = jnp.concatenate([pair[:, 64:128], pair[:, 0:64]], axis=1)
-    qcat[0, :, :, :, LAT:] = split(jnp.where(iota((ROWS, 128), 1) // 64 == h_, pair, swapped))
-
-    to_smem.wait()
-    pl.semaphore_wait(barrier, len(greet))
-
-    query = {}
-    for steps, place in ((1, 3), (3, 2), (2, 1)):
-        query[place] = pltpu.make_async_remote_copy(
-            src_ref=qcat.at[0, :, core],
-            dst_ref=qcat.at[place, :, core],
-            send_sem=q_send,
-            recv_sem=q_recv.at[place],
-            device_id=peer(0, steps),
-            device_id_type=MESH,
-        )
-        query[place].start()
 
     loads[5].wait()
     for i in range(32):
         rope_f[PAGES * i : PAGES * i + PAGES, :] = rope_v[:, 128 * i : 128 * i + 128].astype(
             jnp.float32
         )
+    to_smem.wait()
     loads[6].wait()
 
     def take(group, j):
@@ -318,15 +317,16 @@
         sums, top, total = part
         big = jnp.maximum(jnp.max(jnp.abs(sums), axis=1, keepdims=True), 1e-30)
         steps = jnp.round(sums * (32767.0 / big)).astype(jnp.int32)
-        first = jnp.concatenate([top, total], axis=0)
-        second = jnp.concatenate([big / 32767.0, big], axis=0)
-        stats = jnp.where(lane == 0, first, jnp.where(lane == 1, second, 0.0)).T
-        return steps, stats
+        at, row = iota((PART, 128), 1), iota((PART, 128), 0)
+        first = jnp.where(at == row, top, jnp.where(at == row + PART, total, 0.0))
+        second = jnp.where(at == row, big * (1.0 / 32767.0), 0.0)
+        return steps, [jnp.sum(v, axis=0, keepdims=True) for v in (first, second)]
 
     def give_back(a, k):
         steps_of, stats = encode(merge(halves(a, k)))
         h_acc[a - 1, k] = steps_of.astype(jnp.int16)
-        h_st[a - 1, k] = stats[0:8, :]
+        row = iota((8, 128), 0)
+        h_st[a - 1, k] = jnp.where(row == 0, stats[0], jnp.where(row == 1, stats[1], 0.0))
         axis, steps = {1: (0, 2), 2: (1, 1), 3: (1, 3)}[a]
         slot = {1: 1, 2: 2, 3: 0}[a]
         for n, (source, target) in enumerate(((h_st, r1_st), (h_acc, r1_acc))):
@@ -343,17 +343,20 @@
         pieces = halves(0, k)
         for n, target in enumerate((r1_st, r1_acc)):
             wait(target.at[k], r1_recv.at[k, n])
+        back = r1_st[k].reshape(24, 128)
+        back = jnp.concatenate([back, jnp.zeros((104, 128), jnp.float32)], axis=0).T
         for slot in range(3):
-            back = jnp.concatenate([r1_st[k, slot], jnp.zeros((120, 128), jnp.float32)], axis=0).T
-            values = r1_acc[k, slot].astype(jnp.int32).astype(jnp.float32) * back[0:PART, 1:2]
-            pieces.append((values, back[0:PART, 0:1], back[PART:, 0:1]))
+            i = 8 * slot
+            values = r1_acc[k, slot].astype(jnp.int32).astype(jnp.float32)
+            values = values * back[0:PART, i + 1 : i + 2]
+            pieces.append((values, back[0:PART, i : i + 1], back[PART:, i : i + 1]))
         steps_of, stats = encode(merge(pieces))
         blocks = steps_of.reshape(8, 8, LAT)
         z_out[k] = jnp.concatenate([blocks[:, :, 0:256], blocks[:, :, 256:512]], axis=1).astype(
             jnp.int16
         )
         for n in range(2):
-            z_stat[k, n] = stats[n : n + 1, :]
+            z_stat[k, n] = stats[n]
         for n in range(2):
             for steps in (FAR, NEAR)[k]:
                 copy = pltpu.make_async_remote_copy(
@@ -366,18 +369,33 @@
                 )
                 copy.start()
 
-    for a in (1, 2, 3, 0):
+    def arrived(a):
         if a:
             passed[a].wait_recv()
         wait(kv.at[a, :, 1:4], kv_recv.at[a])
         wait(kr.at[a, :, 1:4], kr_recv.at[a])
         expand_keys(a)
+
+    def both(a):
+        arrived(a)
         for k in range(2):
             attend(a, k)
             swap(a, k)
-        if a:
-            give_back(a, 0)
-            give_back(a, 1)
+
+    both(1)
+    give_back(1, 0)
+    both(2)
+    give_back(2, 0)
+    both(3)
+    give_back(3, 0)
+    arrived(0)
+    attend(0, 0)
+    swap(0, 0)
+    give_back(1, 1)
+    give_back(2, 1)
+    give_back(3, 1)
+    attend(0, 1)
+    swap(0, 1)
     finish(0)
     finish(1)
 
@@ -447,7 +465,7 @@
             pltpu.VMEM((4, 64 * ROPE), bf16),
             pltpu.VMEM((PAGES, TOK, LAT), bf16),
             pltpu.VMEM((PAGES, TOK * ROPE), bf16),
-            pltpu.VMEM((32 * PAGES, 128), f32),
+            pltpu.VMEM((33 * PAGES, 128), f32),
             pltpu.VMEM((16, MAXP), i32),
             pltpu.VMEM((16, MAXP), i32),
             pltpu.VMEM((32, 128), i32),

time: 60.6 us -> 60.5 us (level); the launches traced: 60.5 us -> 59.6 us
  Pallas kernels: 59.8 us -> 59 us
    pallas_call x1, Pallas kernels: 58.5 us -> 57.7 us  [per_device(): pl.pallas_call(kernel, out_shape=jax.ShapeDtypeStruct((8, LAT + 128), f32...]
where the time goes in v4:
time: 60.5 us; the launch traced here: 59.6 us
  Pallas kernels  59 us (98%)
  between operations  0.64 us (1%)
    pallas_call x1, Pallas kernels, per_device(): pl.pallas_call(kernel, out_shape=jax.ShapeDtypeStruct((8, LAT + 128), f32...  57.7 us
    pallas_call x1, Pallas kernels, per_device(): pl.pallas_call(layout_kernel, out_shape=(jax.ShapeDtypeStruct((4, 2, LAT)...  1.34 us

profile of v4, /device:TPU:1, one launch (start us, length us, event | category | flops | bytes accessed | tf_op | source)
XLA Modules:
  0.0 59.6 jit_solution(18111017241173282463)
XLA Ops:
  0.6 57.7 %shard_map.86.rows = f32[8,640]{1,0:T(8,128)} custom-call(s32[16]{0:T(128)} %slot_hbm.1, s32[16]{0:T(128)} %len_hbm.1, s32[16,1536]{1,0:T(8,128)} %table_hbm.1, bf16[256,512]{1,0:T(8,128)(2,1)} %bitcast.6, bf16[4,4096]{1,0:T(4,128)(2,1)} %bitcast.7, bf16[48,64,512]{2,1,0:T(8,128)(2,1)} %lat_hbm.1, bf16[48,4096]{1,0:T(8,128)(2,1)} %rope_hbm.1), custom_call_target="tpu_custom_call" | custom-call | flops 2000000000 | bytes 4000000 | tf_op jit(solution)/shard_map/pallas_call | solution.py:455
  58.3 1.3 %shard_map.87 = (bf16[4,2,512]{2,1,0:T(2,128)(2,1)}, f32[2,4]{1,0:T(2,128)}) custom-call(f32[8,640]{1,0:T(8,128)} %shard_map.86.rows), custom_call_target="tpu_custom_call" | custom-call | tf_op jit(solution)/shard_map/pallas_call | solution.py:523
